TPU v7x, 32 devices: a whole 2x2x4 slice. The times are simulated.
32 devices in a mesh: gx: 2 (over y), gy: 4 (over x, core), gz: 4 (over z).
Axes of the slice: x: 2, y: 2, z: 4, core: 2. Of those that a mesh axis runs over, the one named last changes fastest.
Arguments:
- bricks: bfloat16 [256, 2, 128, 128], P(('gx', 'gy', 'gz')), may hold values from -6 to 6
- live: int32 [256], P(('gx', 'gy', 'gz')), may hold values from 1 to 2, as said below
- shear: float32 [4, 2], replicated, may hold values from -1 to 1
- offsets: int32 [256, 4, 2], P(('gx', 'gy', 'gz')), may hold values from -8 to 8
- absorb: bfloat16 [256], P(('gx', 'gy', 'gz')), may hold values from 0.019897461 to 0.119628906
- color_gain: float32 [3], replicated, may hold values from 0.5 to 3
- color_bias: float32 [3], replicated, may hold values from -1 to 1
- targets: int32 [256, 4], P(('gx', 'gy', 'gz')), may hold values from 0 to 63, as said below
- order: int32 [4, 256], P(None, ('gx', 'gy', 'gz')), may hold values from 0 to 255, each once within a row
Outputs:
- image: float32 [64, 4, 128, 128], P(('gx', 'gy', 'gz'))
Inputs may be any that keep to these rules, and one draw needn't show every extreme that they name: Slices from live[b] on are empty; a device's rendering load can be up to twice another's. targets[b, v] = u has u mod 4 = v; tile u is owned by device u // 2 (devices counted in mesh order) and brick b by device b // 8, and both devices have the same gx index. A device sends at most 2 footprints to any one device; for each gx index some device receives 2 footprints from every device with that gx index. order[v] is a permutation of the bricks.
All inputs are finite; a program needn't handle non-finite values.
Results may differ from a plain program's by a relative error of at most 0.0016.
Values may be sent and summed in bfloat16 or wider, within the bound.
A program may use at most 64 MiB of HBM per device.

v0:
```python
import math

import jax
import jax.numpy as jnp
from jax import lax
from jax.sharding import PartitionSpec as P


def interp_rows(shifted, extent):
    places = jnp.arange(extent, dtype=jnp.float32)
    spacing = places[:, None] - places[None, :] - shifted
    return jnp.maximum(0.0, 1.0 - jnp.abs(spacing)).astype(jnp.bfloat16)


def render_brick(brick, live_count, absorb_rate, offset_rows, shear, color_gain, color_bias):
    extent = brick.shape[-1]
    layers = brick.shape[0]
    views_all = shear.shape[0]
    offset_float = offset_rows.astype(jnp.float32)
    strength = absorb_rate.astype(jnp.float32)
    make_rows = jax.vmap(lambda shifted: interp_rows(shifted, extent))

    def advance(position, carry):
        colors, optical = carry
        layer = lax.dynamic_index_in_dim(brick, position, 0, keepdims=False)
        raised = position.astype(jnp.float32) - jnp.float32(layers // 2)
        shifted = offset_float + raised * shear
        across = make_rows(shifted[:, 0])
        downward = make_rows(shifted[:, 1])
        halfway = jnp.einsum(
            "vij,jk->vik", across, layer, preferred_element_type=jnp.float32
        ).astype(jnp.bfloat16)
        density = jnp.einsum("vik,vlk->vil", halfway, downward, preferred_element_type=jnp.float32)
        thickness = strength * jax.nn.softplus(density)
        emitted = (1.0 - jnp.exp(-thickness))[:, None] * jax.nn.sigmoid(
            color_gain[None, :, None, None] * density[:, None] + color_bias[None, :, None, None]
        )
        return (colors + jnp.exp(-optical)[:, None] * emitted, optical + thickness)

    start = (
        jnp.zeros((views_all, 3, extent, extent), jnp.float32),
        jnp.zeros((views_all, extent, extent), jnp.float32),
    )
    colors, optical = lax.fori_loop(0, live_count, advance, start)
    return (colors.astype(jnp.bfloat16), optical.astype(jnp.bfloat16))


def render_group(bricks, lives, absorb, offsets, shear, color_gain, color_bias):

    def single(inputs):
        brick, live_count, absorb_rate, offset_rows = inputs
        return render_brick(
            brick, live_count, absorb_rate, offset_rows, shear, color_gain, color_bias
        )

    return lax.map(single, (bricks, lives, absorb, offsets))


def composite(recv_color, recv_depth, tile_label, rank_label):
    slots_all = recv_depth.shape[0]
    extent = recv_depth.shape[-1]
    pixels = extent * extent
    block_width = math.gcd(pixels, 4096)
    block_count = pixels // block_width
    flat_color = recv_color.reshape(slots_all, 3, pixels)
    flat_depth = recv_depth.reshape(slots_all, pixels)
    earlier = (
        (tile_label[:, None] == tile_label[None, :])
        & (rank_label[None, :] < rank_label[:, None])
        & (tile_label[None, :] >= 0)
    ).astype(jnp.float32)
    select = (tile_label[None, :] == jnp.arange(2, dtype=jnp.int32)[:, None]).astype(jnp.float32)

    def one_block(begin):
        depth_part = lax.dynamic_slice_in_dim(flat_depth, begin, block_width, 1).astype(jnp.float32)
        color_part = lax.dynamic_slice_in_dim(flat_color, begin, block_width, 2).astype(jnp.float32)
        prefix = jnp.dot(
            earlier, depth_part, precision=lax.Precision.HIGHEST, preferred_element_type=jnp.float32
        )
        shaded = jnp.einsum(
            "tr,rcp->tcp",
            select,
            jnp.exp(-prefix)[:, None] * color_part,
            precision=lax.Precision.HIGHEST,
        )
        cleared = jnp.exp(
            -jnp.dot(
                select,
                depth_part,
                precision=lax.Precision.HIGHEST,
                preferred_element_type=jnp.float32,
            )
        )
        return jnp.concatenate([shaded, cleared[:, None]], axis=1)

    blocks_out = lax.map(one_block, jnp.arange(block_count, dtype=jnp.int32) * block_width)
    return blocks_out.transpose(1, 2, 0, 3).reshape(2, 4, extent, extent)


def body(bricks, live, shear, offsets, absorb, color_gain, color_bias, targets, order):
    brick_count = bricks.shape[0]
    views_all = shear.shape[0]
    extent = bricks.shape[-1]
    colors, optical = render_group(bricks, live, absorb, offsets, shear, color_gain, color_bias)
    item_count = brick_count * views_all
    row_size = lax.axis_size(("gy", "gz"))
    capacity = (item_count + row_size - 1) // row_size
    slots_all = row_size * capacity
    dest_tile = targets.reshape(item_count)
    dest_device = dest_tile // 2 % row_size
    local_tile = dest_tile % 2
    rank_items = order.T.reshape(item_count)
    item_index = jnp.arange(item_count)
    preceding = (dest_device[:, None] == dest_device[None, :]) & (
        item_index[None, :] < item_index[:, None]
    )
    copy_index = jnp.sum(preceding.astype(jnp.int32), axis=1)
    slot_index = dest_device * capacity + copy_index
    send_color = (
        jnp.zeros((slots_all, 3, extent, extent), jnp.bfloat16)
        .at[slot_index]
        .set(colors.reshape(item_count, 3, extent, extent))
    )
    send_depth = (
        jnp.zeros((slots_all, extent, extent), jnp.bfloat16)
        .at[slot_index]
        .set(optical.reshape(item_count, extent, extent))
    )
    send_tile = jnp.full((slots_all,), -1, jnp.int32).at[slot_index].set(local_tile)
    send_rank = jnp.zeros((slots_all,), jnp.int32).at[slot_index].set(rank_items)
    recv_color, recv_depth, recv_tile, recv_rank = (
        lax.all_to_all(send_color, ("gy", "gz"), split_axis=0, concat_axis=0, tiled=True),
        lax.all_to_all(send_depth, ("gy", "gz"), split_axis=0, concat_axis=0, tiled=True),
        lax.all_to_all(send_tile, ("gy", "gz"), split_axis=0, concat_axis=0, tiled=True),
        lax.all_to_all(send_rank, ("gy", "gz"), split_axis=0, concat_axis=0, tiled=True),
    )
    return composite(recv_color, recv_depth, recv_tile, recv_rank)


def solution(mesh):
    placed = (
        P(("gx", "gy", "gz"), None, None, None),
        P(("gx", "gy", "gz")),
        P(),
        P(("gx", "gy", "gz"), None, None),
        P(("gx", "gy", "gz")),
        P(),
        P(),
        P(("gx", "gy", "gz"), None),
        P(None, ("gx", "gy", "gz")),
    )
    return jax.shard_map(
        body,
        mesh=mesh,
        in_specs=placed,
        out_specs=P(("gx", "gy", "gz"), None, None, None),
        check_vma=False,
    )
```

profile of v0, /device:TPU:3, one launch (start us, length us, event | category | flops | bytes accessed | tf_op | source)
XLA Modules:
  0.0 254.9 jit_solution(7997526681979169718)
XLA Ops:
  2.5 6.7 %all-to-all-start.1 = ((s32[16,2,1]{1,2,0:T(1,128)}), s32[16,2,1]{1,2,0:T(1,128)S(1)}, u32[]{:S(2)}, u32[]{:S(2)}) async-start(s32[16,2,1]{1,2,0:T(1,128)} %bitcast.14), calls=%async_computation.1 | async-start | bytes 16384 | tf_op jit(solution)/shard_map/all_to_all | solution.py:134
  10.0 87.1 %while.51 = (s32[]{:T(128)}, bf16[8,4,3,128,128]{4,3,2,1,0:T(8,128)(2,1)}, bf16[8,4,128,128]{3,2,1,0:T(8,128)(2,1)S(1)}, s32[8]{0:T(128)}, bf16[8,2,128,128]{3,2...) while((s32[]{:T(128)}, ...), condition=%wide.region_4.5_spmd, body=%wide.region_1.4_spmd.sunk | while | flops 36847648 | bytes 6654210 | solution.py:56
  14.1 3.6 %while.53 = (s32[]{:T(128)}, f32[4,3,128,128]{3,2,1,0:T(8,128)S(1)}, f32[4,128,128]{2,1,0:T(8,128)S(1)}, s32[]{:T(128)}, f32[]{:T(128)}, /*index=5*/f32[4,2]{0,1...) while((s32[]{:T(128)}, ...), condition=%wide.region_3.3_spmd, body=%wide.region_2.2_spmd.sunk | while | flops 36585496 | bytes 3900799 | solution.py:44
  22.7 6.7 %while.53 = (s32[]{:T(128)}, f32[4,3,128,128]{3,2,1,0:T(8,128)S(1)}, f32[4,128,128]{2,1,0:T(8,128)S(1)}, s32[]{:T(128)}, f32[]{:T(128)}, /*index=5*/f32[4,2]{0,1...) while((s32[]{:T(128)}, ...), condition=%wide.region_3.3_spmd, body=%wide.region_2.2_spmd.sunk | while | flops 36585496 | bytes 3900799 | solution.py:44
  34.3 6.7 %while.53 = (s32[]{:T(128)}, f32[4,3,128,128]{3,2,1,0:T(8,128)S(1)}, f32[4,128,128]{2,1,0:T(8,128)S(1)}, s32[]{:T(128)}, f32[]{:T(128)}, /*index=5*/f32[4,2]{0,1...) while((s32[]{:T(128)}, ...), condition=%wide.region_3.3_spmd, body=%wide.region_2.2_spmd.sunk | while | flops 36585496 | bytes 3900799 | solution.py:44
  45.9 6.7 %while.53 = (s32[]{:T(128)}, f32[4,3,128,128]{3,2,1,0:T(8,128)S(1)}, f32[4,128,128]{2,1,0:T(8,128)S(1)}, s32[]{:T(128)}, f32[]{:T(128)}, /*index=5*/f32[4,2]{0,1...) while((s32[]{:T(128)}, ...), condition=%wide.region_3.3_spmd, body=%wide.region_2.2_spmd.sunk | while | flops 36585496 | bytes 3900799 | solution.py:44
  57.6 6.7 %while.53 = (s32[]{:T(128)}, f32[4,3,128,128]{3,2,1,0:T(8,128)S(1)}, f32[4,128,128]{2,1,0:T(8,128)S(1)}, s32[]{:T(128)}, f32[]{:T(128)}, /*index=5*/f32[4,2]{0,1...) while((s32[]{:T(128)}, ...), condition=%wide.region_3.3_spmd, body=%wide.region_2.2_spmd.sunk | while | flops 36585496 | bytes 3900799 | solution.py:44
  69.2 6.7 %while.53 = (s32[]{:T(128)}, f32[4,3,128,128]{3,2,1,0:T(8,128)S(1)}, f32[4,128,128]{2,1,0:T(8,128)S(1)}, s32[]{:T(128)}, f32[]{:T(128)}, /*index=5*/f32[4,2]{0,1...) while((s32[]{:T(128)}, ...), condition=%wide.region_3.3_spmd, body=%wide.region_2.2_spmd.sunk | while | flops 36585496 | bytes 3900799 | solution.py:44
  80.9 3.6 %while.53 = (s32[]{:T(128)}, f32[4,3,128,128]{3,2,1,0:T(8,128)S(1)}, f32[4,128,128]{2,1,0:T(8,128)S(1)}, s32[]{:T(128)}, f32[]{:T(128)}, /*index=5*/f32[4,2]{0,1...) while((s32[]{:T(128)}, ...), condition=%wide.region_3.3_spmd, body=%wide.region_2.2_spmd.sunk | while | flops 36585496 | bytes 3900799 | solution.py:44
  89.5 6.7 %while.53 = (s32[]{:T(128)}, f32[4,3,128,128]{3,2,1,0:T(8,128)S(1)}, f32[4,128,128]{2,1,0:T(8,128)S(1)}, s32[]{:T(128)}, f32[]{:T(128)}, /*index=5*/f32[4,2]{0,1...) while((s32[]{:T(128)}, ...), condition=%wide.region_3.3_spmd, body=%wide.region_2.2_spmd.sunk | while | flops 36585496 | bytes 3900799 | solution.py:44
  98.6 6.0 %all-to-all-start.2 = ((s32[16,2,1]{1,2,0:T(1,128)}), s32[16,2,1]{1,2,0:T(1,128)S(1)}, u32[]{:S(2)}, u32[]{:S(2)}) async-start(s32[16,2,1]{1,2,0:T(1,128)} %bitcast.16), calls=%async_computation.2 | async-start | bytes 16384 | tf_op jit(solution)/shard_map/all_to_all | solution.py:135
  105.9 4.6 %scatter_fusion = bf16[32,128,128]{2,1,0:T(8,128)(2,1)} fusion(bf16[32,128,128]{2,1,0:T(8,128)(2,1)} %broadcast_in_dim.41, s32[32]{0:T(128)S(1)} %fusion.58, bf16[32,128,128]{2,1,0:T(8,128)(2,1)S(1)} %bitcast.91), kind=kCustom, calls=%fused_computation | custom fusion | bytes 3145856 | tf_op jit(solution)/shard_map/scatter | solution.py:127
  110.4 6.1 %all-to-all-start = ((bf16[32,128,128]{2,1,0:T(8,128)(2,1)}), bf16[32,128,128]{2,1,0:T(8,128)(2,1)S(1)}, u32[]{:S(2)}, u32[]{:S(2)}) async-start(bf16[32,128,128]{2,1,0:T(8,128)(2,1)} %scatter_fusion), calls=%async_computation | async-start | bytes 2097152 | tf_op jit(solution)/shard_map/all_to_all | solution.py:133
  116.5 2.5 broadcast_in_dim.44
  119.0 10.4 %scatter_fusion.1 = bf16[32,3,128,128]{3,2,1,0:T(8,128)(2,1)} fusion(bf16[32,3,128,128]{3,2,1,0:T(8,128)(2,1)} %broadcast_in_dim.44, s32[32]{0:T(128)S(1)} %fusion.58, bf16[32,3,128,128]{3,2,1,0:T(8,128)(2,1)} %bitcast.90), kind=kCustom, calls=%fused_computation.3 | custom fusion | bytes 9437312 | tf_op jit(solution)/shard_map/scatter | solution.py:122
  129.3 12.9 %all-to-all-done = bf16[32,128,128]{2,1,0:T(8,128)(2,1)S(1)} async-done(((bf16[32,128,128]{2,1,0:T(8,128)(2,1)}), bf16[32,128,128]{2,1,0:T(8,128)(2,1)S(1)}, u32[]{:S(2)}, u32[]{:S(2)}) %all-to-all-start) | async-done | bytes 1048608 | tf_op jit(solution)/shard_map/all_to_all | solution.py:133
  143.3 4.9 %all-to-all-start.3 = ((bf16[32,3,128,128]{3,2,1,0:T(8,128)(2,1)}), bf16[32,3,128,128]{3,2,1,0:T(8,128)(2,1)S(1)}, u32[]{:S(2)}, u32[]{:S(2)}) async-start(bf16[32,3,128,128]{3,2,1,0:T(8,128)(2,1)} %scatter_fusion.1), calls=%async_computation.3 | async-start | bytes 6291456 | tf_op jit(solution)/shard_map/all_to_all | solution.py:132
  150.2 2.9 %copy.45 = bf16[4,8,128,128]{3,1,2,0:T(8,128)(2,1)} copy(bf16[4,8,128,128]{3,2,1,0:T(8,128)(2,1)} %bitcast.89) | data formatting | bytes 2097152
  153.1 65.8 %all-to-all-done.3 = bf16[32,3,128,128]{3,2,1,0:T(8,128)(2,1)S(1)} async-done(((bf16[32,3,128,128]{3,2,1,0:T(8,128)(2,1)}), bf16[32,3,128,128]{3,2,1,0:T(8,128)(2,1)S(1)}, u32[]{:S(2)}, u32[]{:S(2)}) %all-to-all-start.3) | async-done | bytes 3145760 | tf_op jit(solution)/shard_map/all_to_all | solution.py:132
  218.9 1.8 copy.38
  220.7 4.1 %reshape.240 = bf16[32,3,16384]{2,0,1:T(8,128)(2,1)S(1)} reshape(bf16[32,3,128,128]{3,2,0,1:T(8,128)(2,1)} %copy.38) | data formatting | bytes 6291456 | tf_op jit(solution)/shard_map/reshape | solution.py:65
  224.9 27.5 %while.52 = (s32[]{:T(128)}, f32[4,2,4,4096]{3,1,2,0:T(2,128)}, s32[4]{0:T(128)S(1)}, bf16[32,16384]{1,0:T(8,128)(2,1)}, bf16[32,3,16384]{2,0,1:T(8,128)(2,1)S(1...) while((s32[]{:T(128)}, f32[4,2,4,4096]{3,1,2,0:T(2,128)}, ...), condition=%wide.region_10.11_spmd.clone.clone, body=%wide.region_9.10_spmd.clone.clone.sunk | while | flops 63878404 | bytes 2756391 | solution.py:96
  227.1 1.4 fusion.81
  240.9 1.4 fusion.81
  (184 shorter events, 98.0 us)
Async XLA Ops:
  2.5 96.1 %all-to-all-start.1 = ((s32[16,2,1]{1,2,0:T(1,128)}), s32[16,2,1]{1,2,0:T(1,128)S(1)}, u32[]{:S(2)}, u32[]{:S(2)}) async-start(s32[16,2,1]{1,2,0:T(1,128)} %bitcast.14), calls=%async_computation.1 | async-start | bytes 16384 | tf_op jit(solution)/shard_map/all_to_all | solution.py:134
  10.0 87.1 %copy-start.1 = (s32[4,8]{1,0:T(4,128)S(1)}, s32[4,8]{1,0:T(4,128)}, u32[]{:S(2)}) copy-start(s32[4,8]{1,0:T(4,128)} %param.23) | copy-start | bytes 388
  98.6 11.8 %all-to-all-start.2 = ((s32[16,2,1]{1,2,0:T(1,128)}), s32[16,2,1]{1,2,0:T(1,128)S(1)}, u32[]{:S(2)}, u32[]{:S(2)}) async-start(s32[16,2,1]{1,2,0:T(1,128)} %bitcast.16), calls=%async_computation.2 | async-start | bytes 16384 | tf_op jit(solution)/shard_map/all_to_all | solution.py:135
  110.4 31.8 %all-to-all-start = ((bf16[32,128,128]{2,1,0:T(8,128)(2,1)}), bf16[32,128,128]{2,1,0:T(8,128)(2,1)S(1)}, u32[]{:S(2)}, u32[]{:S(2)}) async-start(bf16[32,128,128]{2,1,0:T(8,128)(2,1)} %scatter_fusion), calls=%async_computation | async-start | bytes 2097152 | tf_op jit(solution)/shard_map/all_to_all | solution.py:133
  142.3 1.0 copy-start
  143.3 75.6 %all-to-all-start.3 = ((bf16[32,3,128,128]{3,2,1,0:T(8,128)(2,1)}), bf16[32,3,128,128]{3,2,1,0:T(8,128)(2,1)S(1)}, u32[]{:S(2)}, u32[]{:S(2)}) async-start(bf16[32,3,128,128]{3,2,1,0:T(8,128)(2,1)} %scatter_fusion.1), calls=%async_computation.3 | async-start | bytes 6291456 | tf_op jit(solution)/shard_map/all_to_all | solution.py:132
where the time goes:
time: 259 us; the launch traced here: 255 us
  waiting for transfers between devices  78.7 us (30%)
  local copies, waits for them, and re-layouts  66.2 us (26%)
  other arithmetic  37.8 us (15%)
  loops' own time  25.3 us (10%)
  starting transfers between devices  23.6 us (9%)
  matrix products  23.1 us (9%)
    all_to_all x1, waiting for transfers between devices, body(): lax.all_to_all(send_color, ('gy', 'gz'), split_axis=0, concat_axis=0, til...  65.8 us
    dynamic_slice x16, local copies, waits for them, and re-layouts, render_group(): return lax.map(single, (bricks, lives, absorb, offsets))  20 us
    add x14, other arithmetic, advance(): return (colors + jnp.exp(-optical)[:, None] * emitted, optical + thickness)  16.5 us
    another operation x8, loops' own time, render_brick(): colors, optical = lax.fori_loop(0, live_count, advance, start)  13.1 us
    all_to_all x1, waiting for transfers between devices, body(): lax.all_to_all(send_depth, ('gy', 'gz'), split_axis=0, concat_axis=0, til...  12.9 us
    scatter x1, local copies, waits for them, and re-layouts, body(): send_color = jnp.zeros((slots_all, 3, extent, extent), jnp.bfloat16).at[s...  10.4 us
    add x14, other arithmetic, advance(): shifted = offset_float + raised * shear  9.59 us
    dot_general x14, matrix products, advance(): jnp.einsum('vik,vlk->vil', halfway, downward, preferred_element_type=jnp....  7.71 us
  transfers between devices with their start and end apart: 4, of which 2 were waited for; matrix products, arithmetic and copies ran while one was open for 37% of the time, Pallas kernels for 0%

commit v1 on v0

v1 whole, which is shorter than its diff:
```python
import functools

import jax
import jax.numpy as jnp
from jax import lax
from jax.experimental import pallas as pl
from jax.experimental.pallas import tpu as pltpu
from jax.sharding import PartitionSpec as P

MESH = pl.DeviceIdType.MESH
F32 = jnp.float32
BF16 = jnp.bfloat16
LANES = 128
ABSORB_UNIT = float(2**20)
OFF_X, OFF_Y, LIVE, VIEW, ABSORB, TILE, RANK, BRICK = range(8)


def table_kernel(row, capacity, targets, offsets, live, absorb, order, table, counts):
    bricks, views = targets.shape

    def clear(d, _):
        counts[d] = 0
        for c in range(capacity):
            for field in range(8):
                table[d, c, field] = -1 if field == TILE else 0
        return 0

    lax.fori_loop(0, row, clear, 0)

    def place(b, _):
        for v in range(views):
            tile = targets[b, v]
            d = lax.rem(lax.div(tile, 2), row)
            c = counts[d]
            counts[d] = c + 1
            table[d, c, OFF_X] = offsets[b, 2 * v]
            table[d, c, OFF_Y] = offsets[b, 2 * v + 1]
            table[d, c, LIVE] = live[b]
            table[d, c, VIEW] = v
            table[d, c, ABSORB] = absorb[b]
            table[d, c, TILE] = lax.rem(tile, 2)
            table[d, c, RANK] = order[v, b]
            table[d, c, BRICK] = b
        return 0

    lax.fori_loop(0, bricks, place, 0)


def main_kernel(
    ny, nz, capacity,
    table_s, table_v, bricks, shear, gain, bias,
    out,
    send_buf, recv_buf, recv_table, recv_scalar, sort_v, sort_s, spacing, foot, keys,
    table_send, table_recv, brick_send, brick_recv, local_sem,
):
    row = ny * nz
    slots = row * capacity
    layers, extent = bricks.shape[1], bricks.shape[2]
    my_y, my_z = lax.axis_index("gy"), lax.axis_index("gz")
    steps = [(0, 0)] + [
        (dy, dz)
        for dz in sorted(range(nz), key=lambda dz: -min(dz, nz - dz))
        for dy in range(ny)
        if (dy, dz) != (0, 0)
    ]

    def peer(e):
        dy, dz = steps[e]
        return lax.rem(my_y + dy, ny), lax.rem(my_z + dz, nz)

    barrier = pltpu.get_barrier_semaphore()
    for e in range(1, row):
        py, pz = peer(e)
        pl.semaphore_signal(barrier, inc=1, device_id={"gy": py, "gz": pz}, device_id_type=MESH)

    def table_copy(e, py, pz):
        return pltpu.make_async_remote_copy(
            src_ref=table_v.at[py * nz + pz], dst_ref=recv_table.at[e],
            send_sem=table_send.at[e], recv_sem=table_recv.at[e],
            device_id={"gy": py, "gz": pz}, device_id_type=MESH,
        )

    def brick_copy(e, py, pz):
        return pltpu.make_async_remote_copy(
            src_ref=send_buf.at[e], dst_ref=recv_buf.at[e],
            send_sem=brick_send.at[e], recv_sem=brick_recv.at[e],
            device_id={"gy": py, "gz": pz}, device_id_type=MESH,
        )

    def gather(e, py, pz, into):
        for c in range(capacity):
            into[e, c] = bricks[table_s[py * nz + pz, c, BRICK]]

    gather(1, *peer(1), send_buf)
    pl.semaphore_wait(barrier, row - 1)
    for e in range(1, row):
        table_copy(e, *peer(e)).start()
    for e in range(1, row):
        py, pz = peer(e)
        if e > 1:
            gather(e, py, pz, send_buf)
        brick_copy(e, py, pz).start()

    gather(0, my_y, my_z, recv_buf)
    recv_table[0] = table_v[my_y * nz + my_z]
    rows = lax.broadcasted_iota(jnp.int32, (extent, extent), 0)
    cols = lax.broadcasted_iota(jnp.int32, (extent, extent), 1)
    spacing[...] = (rows - cols).astype(F32)

    def table_arrived(e, _):
        table_copy(e, my_y, my_z).wait_recv()
        return 0

    lax.fori_loop(1, row, table_arrived, 0)
    to_scalar = pltpu.make_async_copy(recv_table, recv_scalar, local_sem.at[0])
    to_scalar.start()

    keys[...] = jnp.full(keys.shape, -1, jnp.int32)
    for e in range(row):
        keys[e * capacity:(e + 1) * capacity, :] = recv_table[e, 0:capacity, :]
    tile = keys[:, TILE:TILE + 1]
    key = jnp.where(tile < 0, 2, tile) * (1 << 20) + keys[:, RANK:RANK + 1]
    size = keys.shape[0]
    key = jnp.broadcast_to(key, (size, size))
    other = key.T
    me = lax.broadcasted_iota(jnp.int32, (size, size), 0)
    it = lax.broadcasted_iota(jnp.int32, (size, size), 1)
    ahead = (other < key) | ((other == key) & (it < me))
    place = jnp.sum(jnp.where(ahead, 1, 0), axis=1, keepdims=True)
    hit = place == it
    sort_v[0:1, :] = jnp.sum(jnp.where(hit, me, 0), axis=0, keepdims=True)
    sort_v[1:2, :] = jnp.sum(jnp.where(hit & (tile == 0), 1, 0), axis=0, keepdims=True)
    sort_v[2:3, :] = jnp.sum(jnp.where(hit & (tile == 1), 1, 0), axis=0, keepdims=True)
    to_sort = pltpu.make_async_copy(sort_v, sort_s, local_sem.at[1])
    to_sort.start()
    to_scalar.wait()
    to_sort.wait()

    def interp(shifted):
        return jnp.maximum(0.0, 1.0 - jnp.abs(spacing[...] - shifted)).astype(BF16)

    def render(e):
        for c in range(capacity):
            off_x = recv_scalar[e, c, OFF_X].astype(F32)
            off_y = recv_scalar[e, c, OFF_Y].astype(F32)
            count = recv_scalar[e, c, LIVE]
            view = recv_scalar[e, c, VIEW]
            strength = recv_scalar[e, c, ABSORB].astype(F32) * (1.0 / ABSORB_UNIT)
            optical, clear, colors = None, None, [None] * 3
            for k in range(layers):
                raised = float(k - layers // 2)
                across = interp(off_x + raised * shear[view, 0])
                downward = interp(off_y + raised * shear[view, 1])
                halfway = jnp.dot(across, recv_buf[e, c, k], preferred_element_type=F32).astype(BF16)
                density = lax.dot_general(
                    halfway, downward, (((1,), (1,)), ((), ())), preferred_element_type=F32
                )
                rate = jnp.where(k < count, strength, 0.0)
                soft = jnp.maximum(density, 0.0) + jnp.log(1.0 + jnp.exp(-jnp.abs(density)))
                thickness = rate * soft
                passed = jnp.exp(-thickness)
                half_alpha = 0.5 - 0.5 * passed
                if k:
                    half_alpha = half_alpha * clear
                for n in range(3):
                    lit = half_alpha + half_alpha * jnp.tanh(
                        (0.5 * gain[n]) * density + 0.5 * bias[n]
                    )
                    colors[n] = lit if k == 0 else colors[n] + lit
                optical = thickness if k == 0 else optical + thickness
                clear = passed if k == 0 else clear * passed
            for n in range(3):
                foot[e * capacity + c, n] = colors[n].astype(BF16)
            foot[e * capacity + c, 3] = optical.astype(BF16)

    render(0)

    def arrived(e, _):
        brick_copy(e, my_y, my_z).wait_recv()
        render(e)
        return 0

    lax.fori_loop(1, row, arrived, 0)

    def left(e, _):
        table_copy(e, my_y, my_z).wait_send()
        brick_copy(e, my_y, my_z).wait_send()
        return 0

    lax.fori_loop(1, row, left, 0)

    height = 16

    def strip(r, _):
        lines = pl.ds(pl.multiple_of(r * height, height), height)

        def visit(p, carry):
            optical0, optical1, color0, color1 = carry
            which = sort_s[0, p]
            in0 = sort_s[1, p].astype(F32)
            in1 = sort_s[2, p].astype(F32)
            clear = jnp.exp(-(optical0 * in0 + optical1 * in1))
            clear0, clear1 = clear * in0, clear * in1
            shade = [foot[which, n, lines, :].astype(F32) for n in range(3)]
            depth = foot[which, 3, lines, :].astype(F32)
            return (
                optical0 + in0 * depth,
                optical1 + in1 * depth,
                tuple(c + clear0 * s for c, s in zip(color0, shade)),
                tuple(c + clear1 * s for c, s in zip(color1, shade)),
            )

        zero = jnp.zeros((height, extent), F32)
        optical0, optical1, color0, color1 = lax.fori_loop(
            0, slots, visit, (zero, zero, (zero,) * 3, (zero,) * 3), unroll=4
        )
        for n in range(3):
            out[0, n, lines, :] = color0[n]
            out[1, n, lines, :] = color1[n]
        out[0, 3, lines, :] = jnp.exp(-optical0)
        out[1, 3, lines, :] = jnp.exp(-optical1)
        return 0

    lax.fori_loop(0, extent // height, strip, 0)


def body(ny, nz, bricks, live, shear, offsets, absorb, color_gain, color_bias, targets, order):
    brick_count, layers, extent, _ = bricks.shape
    views = shear.shape[0]
    row = ny * nz
    capacity = (brick_count * views + row - 1) // row
    slots = row * capacity
    smem = pl.BlockSpec(memory_space=pltpu.SMEM)
    vmem = pl.BlockSpec(memory_space=pltpu.VMEM)
    table_rows = (capacity + 7) // 8 * 8
    sort_size = (slots + LANES - 1) // LANES * LANES
    absorb_units = jnp.round(absorb.astype(F32) * ABSORB_UNIT).astype(jnp.int32)
    table = pl.pallas_call(
        functools.partial(table_kernel, row, capacity),
        out_shape=jax.ShapeDtypeStruct((row, table_rows, LANES), jnp.int32),
        in_specs=[smem] * 5,
        out_specs=smem,
        scratch_shapes=[pltpu.SMEM((row,), jnp.int32)],
    )(targets, offsets.reshape(brick_count, views * 2), live, absorb_units, order)
    return pl.pallas_call(
        functools.partial(main_kernel, ny, nz, capacity),
        out_shape=jax.ShapeDtypeStruct((2, 4, extent, extent), F32),
        in_specs=[smem, vmem, vmem, smem, smem, smem],
        out_specs=vmem,
        scratch_shapes=[
            pltpu.VMEM((row, capacity, layers, extent, extent), BF16),
            pltpu.VMEM((row, capacity, layers, extent, extent), BF16),
            pltpu.VMEM((row, table_rows, LANES), jnp.int32),
            pltpu.SMEM((row, table_rows, LANES), jnp.int32),
            pltpu.VMEM((8, sort_size), jnp.int32),
            pltpu.SMEM((8, sort_size), jnp.int32),
            pltpu.VMEM((extent, extent), F32),
            pltpu.VMEM((slots, 4, extent, extent), BF16),
            pltpu.VMEM((sort_size, LANES), jnp.int32),
            pltpu.SemaphoreType.DMA((row,)),
            pltpu.SemaphoreType.DMA((row,)),
            pltpu.SemaphoreType.DMA((row,)),
            pltpu.SemaphoreType.DMA((row,)),
            pltpu.SemaphoreType.DMA((2,)),
        ],
        compiler_params=pltpu.CompilerParams(
            collective_id=0, has_side_effects=True, vmem_limit_bytes=48 * 1024 * 1024
        ),
    )(table, table, bricks, shear, color_gain, color_bias)


def solution(mesh):
    ny, nz = mesh.shape["gy"], mesh.shape["gz"]
    split = ("gx", "gy", "gz")
    placed = (
        P(split, None, None, None),
        P(split),
        P(),
        P(split, None, None),
        P(split),
        P(),
        P(),
        P(split, None),
        P(None, split),
    )
    return jax.shard_map(
        functools.partial(body, ny, nz),
        mesh=mesh,
        in_specs=placed,
        out_specs=P(split, None, None, None),
        check_vma=False,
    )
```

time: 259 us -> 71.5 us (0.28)
  the two profiles are of different devices: /device:TPU:3 before, /device:TPU:17 now
where the time goes in v1:
time: 71.5 us; the launch traced here: 71.2 us
  Pallas kernels  65.1 us (91%)
  local copies, waits for them, and re-layouts  5.45 us (8%)
    pallas_call x1, Pallas kernels, body(): pl.pallas_call(functools.partial(main_kernel, ny, nz, capacity), out_shap...  61.8 us
    unnamed x17, local copies, waits for them, and re-layouts  4.8 us
    pallas_call x1, Pallas kernels, body(): pl.pallas_call(functools.partial(table_kernel, row, capacity), out_shape=...  3.28 us

profile of v1, /device:TPU:17, one launch (start us, length us, event | category | flops | bytes accessed | tf_op | source)
XLA Modules:
  0.0 71.2 jit_solution(9273992407452941709)
XLA Ops:
  0.0 0.0 copy-start.6
  0.0 0.0 copy-start.4
  0.0 0.7 copy-done.6
  0.7 0.6 round-nearest-even_convert_fusion.absorb
  1.2 0.8 %copy.12.shear = f32[4,2]{1,0:T(4,128)S(1)} copy(f32[4,2]{0,1:T(2,128)} %param.11) | data formatting | bytes 64 | tf_op args[2]
  2.0 0.0 copy-done.4
  2.0 0.0 copy-start.5
  2.0 0.7 copy.11.offsets
  2.7 0.0 copy-done.5
  2.7 0.7 copy.10.targets
  3.4 0.0 copy-start.2
  3.4 0.0 copy-start.3
  3.4 3.3 %shard_map.91.table_s.table_v = s32[16,8,128]{2,1,0:T(8,128)} custom-call(s32[8,4]{1,0:T(8,128)} %copy.10.targets, s32[8,8]{1,0:T(8,128)} %copy.11.offsets, s32[8]{0:T(128)} %live.1, s32[8]{0:T(128)} %round-nearest-even_convert_fusion.absorb, s32[4,8]{1,0:T(4,128)} %order.1), custom_call_target="tpu_custom_call" | custom-call | tf_op jit(solution)/shard_map/pallas_call | solution.py:238
  6.7 0.0 copy-done.2
  6.7 0.0 copy-done.3
  6.7 0.0 copy-start
  6.7 0.8 %copy-done = s32[16,8,128]{2,1,0:T(8,128)S(1)} copy-done((s32[16,8,128]{2,1,0:T(8,128)S(1)}, s32[16,8,128]{2,1,0:T(8,128)}, u32[]{:S(2)}) %copy-start) | copy-done | bytes 65560
  7.5 0.0 copy-start.1
  7.5 1.0 %copy-done.1 = bf16[8,2,128,128]{3,2,1,0:T(8,128)(2,1)S(1)} copy-done((bf16[8,2,128,128]{3,2,1,0:T(8,128)(2,1)S(1)}, bf16[8,2,128,128]{3,2,1,0:T(8,128)(2,1)}, u32[]{:S(2)}) %copy-start.1) | copy-done | bytes 524312
  8.6 61.8 %shard_map.92 = f32[2,4,128,128]{3,2,1,0:T(8,128)S(1)} custom-call(s32[16,8,128]{2,1,0:T(8,128)S(1)} %copy-done, s32[16,8,128]{2,1,0:T(8,128)S(1)} %copy-done, bf16[8,2,128,128]{3,2,1,0:T(8,128)(2,1)S(1)} %copy-done.1, f32[4,2]{1,0:T(4,128)S(1)} %copy.12.shear, f32[3]{0:T(128)S(1)} %copy-done.2, f32[3]{0:T(128)S(1)} %copy-done.3), custom_call_target="tpu_custom_call" | custom-call | tf_op jit(solution)/shard_map/pallas_call | solution.py:245
  70.4 0.8 %copy.14 = f32[2,4,128,128]{3,2,1,0:T(8,128)} copy(f32[2,4,128,128]{3,2,1,0:T(8,128)S(1)} %shard_map.92) | data formatting | bytes 1048576
Async XLA Ops:
  0.0 0.7 copy-start.6
  0.0 2.0 %copy-start.4 = (s32[8,4,2]{0,2,1:T(2,128)S(1)}, s32[8,4,2]{0,2,1:T(2,128)}, u32[]{:S(2)}) copy-start(s32[8,4,2]{0,2,1:T(2,128)} %param.12) | copy-start | bytes 772
  2.0 0.7 copy-start.5
  3.4 3.3 %copy-start.2 = (f32[3]{0:T(128)S(1)}, f32[3]{0:T(128)}, u32[]{:S(2)}) copy-start(f32[3]{0:T(128)} %gain.1) | copy-start | bytes 40
  3.4 3.3 %copy-start.3 = (f32[3]{0:T(128)S(1)}, f32[3]{0:T(128)}, u32[]{:S(2)}) copy-start(f32[3]{0:T(128)} %bias.1) | copy-start | bytes 40
  6.7 0.8 %copy-start = (s32[16,8,128]{2,1,0:T(8,128)S(1)}, s32[16,8,128]{2,1,0:T(8,128)}, u32[]{:S(2)}) copy-start(s32[16,8,128]{2,1,0:T(8,128)} %shard_map.91.table_s.table_v) | copy-start | bytes 196612
  7.5 1.0 %copy-start.1 = (bf16[8,2,128,128]{3,2,1,0:T(8,128)(2,1)S(1)}, bf16[8,2,128,128]{3,2,1,0:T(8,128)(2,1)}, u32[]{:S(2)}) copy-start(bf16[8,2,128,128]{3,2,1,0:T(8,128)(2,1)} %bricks.1) | copy-start | bytes 1572868

commit v2 on v1

--- a/solution.py
+++ b/solution.py
@@ -15,47 +15,19 @@
 OFF_X, OFF_Y, LIVE, VIEW, ABSORB, TILE, RANK, BRICK = range(8)
 
 
-def table_kernel(row, capacity, targets, offsets, live, absorb, order, table, counts):
-    bricks, views = targets.shape
-
-    def clear(d, _):
-        counts[d] = 0
-        for c in range(capacity):
-            for field in range(8):
-                table[d, c, field] = -1 if field == TILE else 0
-        return 0
-
-    lax.fori_loop(0, row, clear, 0)
-
-    def place(b, _):
-        for v in range(views):
-            tile = targets[b, v]
-            d = lax.rem(lax.div(tile, 2), row)
-            c = counts[d]
-            counts[d] = c + 1
-            table[d, c, OFF_X] = offsets[b, 2 * v]
-            table[d, c, OFF_Y] = offsets[b, 2 * v + 1]
-            table[d, c, LIVE] = live[b]
-            table[d, c, VIEW] = v
-            table[d, c, ABSORB] = absorb[b]
-            table[d, c, TILE] = lax.rem(tile, 2)
-            table[d, c, RANK] = order[v, b]
-            table[d, c, BRICK] = b
-        return 0
-
-    lax.fori_loop(0, bricks, place, 0)
-
-
 def main_kernel(
     ny, nz, capacity,
-    table_s, table_v, bricks, shear, gain, bias,
+    bricks_in, live, shear, offsets, absorb, gain, bias, targets, order,
     out,
-    send_buf, recv_buf, recv_table, recv_scalar, sort_v, sort_s, spacing, foot, keys,
+    bricks, send_buf, recv_buf, send_table, recv_table, raw, items, chosen_v, chosen_s,
+    shift_v, shift_s, sort_v, sort_s, spacing, foot, keys,
     table_send, table_recv, brick_send, brick_recv, local_sem,
 ):
     row = ny * nz
     slots = row * capacity
-    layers, extent = bricks.shape[1], bricks.shape[2]
+    count, layers, extent, _ = bricks.shape
+    views = targets.shape[1]
+    size = keys.shape[0]
     my_y, my_z = lax.axis_index("gy"), lax.axis_index("gz")
     steps = [(0, 0)] + [
         (dy, dz)
@@ -73,9 +45,50 @@
         py, pz = peer(e)
         pl.semaphore_signal(barrier, inc=1, device_id={"gy": py, "gz": pz}, device_id_type=MESH)
 
+    load_bricks = pltpu.make_async_copy(bricks_in, bricks, local_sem.at[0])
+    load_bricks.start()
+
+    raw[...] = jnp.zeros(raw.shape, jnp.int32)
+    raw[0:views, 0:count] = order[...]
+    raw[views:views + 1, 0:count] = live[...]
+    units = jnp.round(absorb[...].astype(F32) * ABSORB_UNIT)
+    raw[views + 1:views + 2, 0:count] = units.astype(jnp.int32)
+    turned = raw[...].T
+    items[...] = jnp.zeros(items.shape, jnp.int32)
+    for v in range(views):
+        mine = slice(v * count, (v + 1) * count)
+        items[mine, OFF_X:OFF_Y + 1] = offsets[:, v, :]
+        items[mine, LIVE:LIVE + 1] = turned[0:count, views:views + 1]
+        items[mine, VIEW:VIEW + 1] = jnp.full((count, 1), v, jnp.int32)
+        items[mine, ABSORB:ABSORB + 1] = turned[0:count, views + 1:views + 2]
+        items[mine, TILE:TILE + 1] = targets[:, v:v + 1]
+        items[mine, RANK:RANK + 1] = turned[0:count, v:v + 1]
+        items[mine, BRICK:BRICK + 1] = lax.broadcasted_iota(jnp.int32, (count, 1), 0)
+    me = lax.broadcasted_iota(jnp.int32, (size, size), 0)
+    it = lax.broadcasted_iota(jnp.int32, (size, size), 1)
+    used = views * count
+    owner = jnp.where(me < used, lax.rem(lax.div(items[:, TILE:TILE + 1], 2), row), -1)
+    same = (owner == owner.T) & (it < me)
+    slot = owner * capacity + jnp.sum(jnp.where(same, 1, 0), axis=1, keepdims=True)
+    slot = jnp.where(me < used, slot, -1)
+    chosen_v[0:1, :] = jnp.sum(
+        jnp.where(slot == it, items[:, BRICK:BRICK + 1], 0), axis=0, keepdims=True
+    )
+    load_chosen = pltpu.make_async_copy(chosen_v, chosen_s, local_sem.at[1])
+    load_chosen.start()
+    hit = (slot.T == me)[0:slots, :]
+    lane = lax.broadcasted_iota(jnp.int32, (slots, LANES), 1)
+    table = jnp.where(lane == TILE, -1, 0)
+    entry = jnp.where(lane[0:1, :] == TILE, lax.rem(items[...], 2) + 1, items[...])
+    hit_int = jnp.where(hit, 1, 0)
+    for i in range(used):
+        table = table + hit_int[:, i:i + 1] * entry[i:i + 1, :]
+    for d in range(row):
+        send_table[d, 0:capacity, :] = table[d * capacity:(d + 1) * capacity, :]
+
     def table_copy(e, py, pz):
         return pltpu.make_async_remote_copy(
-            src_ref=table_v.at[py * nz + pz], dst_ref=recv_table.at[e],
+            src_ref=send_table.at[py * nz + pz], dst_ref=recv_table.at[e],
             send_sem=table_send.at[e], recv_sem=table_recv.at[e],
             device_id={"gy": py, "gz": pz}, device_id_type=MESH,
         )
@@ -89,8 +102,10 @@
 
     def gather(e, py, pz, into):
         for c in range(capacity):
-            into[e, c] = bricks[table_s[py * nz + pz, c, BRICK]]
-
+            into[e, c] = bricks[chosen_s[0, (py * nz + pz) * capacity + c]]
+
+    load_bricks.wait()
+    load_chosen.wait()
     gather(1, *peer(1), send_buf)
     pl.semaphore_wait(barrier, row - 1)
     for e in range(1, row):
@@ -102,7 +117,7 @@
         brick_copy(e, py, pz).start()
 
     gather(0, my_y, my_z, recv_buf)
-    recv_table[0] = table_v[my_y * nz + my_z]
+    recv_table[0] = send_table[my_y * nz + my_z]
     rows = lax.broadcasted_iota(jnp.int32, (extent, extent), 0)
     cols = lax.broadcasted_iota(jnp.int32, (extent, extent), 1)
     spacing[...] = (rows - cols).astype(F32)
@@ -112,28 +127,35 @@
         return 0
 
     lax.fori_loop(1, row, table_arrived, 0)
-    to_scalar = pltpu.make_async_copy(recv_table, recv_scalar, local_sem.at[0])
-    to_scalar.start()
-
     keys[...] = jnp.full(keys.shape, -1, jnp.int32)
     for e in range(row):
         keys[e * capacity:(e + 1) * capacity, :] = recv_table[e, 0:capacity, :]
+    view = keys[:, VIEW:VIEW + 1]
+    for axis in range(2):
+        slope = jnp.zeros((size, 1), F32)
+        for v in range(views):
+            slope = jnp.where(view == v, shear[v:v + 1, axis:axis + 1], slope)
+        offset = keys[:, OFF_X + axis:OFF_X + axis + 1].astype(F32)
+        for k in range(layers):
+            shift_v[:, 3 * k + axis:3 * k + axis + 1] = offset + float(k - layers // 2) * slope
+    strength = keys[:, ABSORB:ABSORB + 1].astype(F32) * (1.0 / ABSORB_UNIT)
+    for k in range(layers):
+        shift_v[:, 3 * k + 2:3 * k + 3] = jnp.where(keys[:, LIVE:LIVE + 1] > k, strength, 0.0)
+    to_shift = pltpu.make_async_copy(shift_v, shift_s, local_sem.at[3])
+    to_shift.start()
     tile = keys[:, TILE:TILE + 1]
     key = jnp.where(tile < 0, 2, tile) * (1 << 20) + keys[:, RANK:RANK + 1]
-    size = keys.shape[0]
     key = jnp.broadcast_to(key, (size, size))
     other = key.T
-    me = lax.broadcasted_iota(jnp.int32, (size, size), 0)
-    it = lax.broadcasted_iota(jnp.int32, (size, size), 1)
     ahead = (other < key) | ((other == key) & (it < me))
     place = jnp.sum(jnp.where(ahead, 1, 0), axis=1, keepdims=True)
     hit = place == it
     sort_v[0:1, :] = jnp.sum(jnp.where(hit, me, 0), axis=0, keepdims=True)
     sort_v[1:2, :] = jnp.sum(jnp.where(hit & (tile == 0), 1, 0), axis=0, keepdims=True)
     sort_v[2:3, :] = jnp.sum(jnp.where(hit & (tile == 1), 1, 0), axis=0, keepdims=True)
-    to_sort = pltpu.make_async_copy(sort_v, sort_s, local_sem.at[1])
+    to_sort = pltpu.make_async_copy(sort_v, sort_s, local_sem.at[2])
     to_sort.start()
-    to_scalar.wait()
+    to_shift.wait()
     to_sort.wait()
 
     def interp(shifted):
@@ -141,21 +163,16 @@
 
     def render(e):
         for c in range(capacity):
-            off_x = recv_scalar[e, c, OFF_X].astype(F32)
-            off_y = recv_scalar[e, c, OFF_Y].astype(F32)
-            count = recv_scalar[e, c, LIVE]
-            view = recv_scalar[e, c, VIEW]
-            strength = recv_scalar[e, c, ABSORB].astype(F32) * (1.0 / ABSORB_UNIT)
+            spot = e * capacity + c
             optical, clear, colors = None, None, [None] * 3
             for k in range(layers):
-                raised = float(k - layers // 2)
-                across = interp(off_x + raised * shear[view, 0])
-                downward = interp(off_y + raised * shear[view, 1])
+                across = interp(shift_s[spot, 3 * k])
+                downward = interp(shift_s[spot, 3 * k + 1])
                 halfway = jnp.dot(across, recv_buf[e, c, k], preferred_element_type=F32).astype(BF16)
                 density = lax.dot_general(
                     halfway, downward, (((1,), (1,)), ((), ())), preferred_element_type=F32
                 )
-                rate = jnp.where(k < count, strength, 0.0)
+                rate = shift_s[spot, 3 * k + 2]
                 soft = jnp.maximum(density, 0.0) + jnp.log(1.0 + jnp.exp(-jnp.abs(density)))
                 thickness = rate * soft
                 passed = jnp.exp(-thickness)
@@ -170,8 +187,8 @@
                 optical = thickness if k == 0 else optical + thickness
                 clear = passed if k == 0 else clear * passed
             for n in range(3):
-                foot[e * capacity + c, n] = colors[n].astype(BF16)
-            foot[e * capacity + c, 3] = optical.astype(BF16)
+                foot[spot, n] = colors[n].astype(BF16)
+            foot[spot, 3] = optical.astype(BF16)
 
     render(0)
 
@@ -233,40 +250,43 @@
     smem = pl.BlockSpec(memory_space=pltpu.SMEM)
     vmem = pl.BlockSpec(memory_space=pltpu.VMEM)
     table_rows = (capacity + 7) // 8 * 8
-    sort_size = (slots + LANES - 1) // LANES * LANES
-    absorb_units = jnp.round(absorb.astype(F32) * ABSORB_UNIT).astype(jnp.int32)
-    table = pl.pallas_call(
-        functools.partial(table_kernel, row, capacity),
-        out_shape=jax.ShapeDtypeStruct((row, table_rows, LANES), jnp.int32),
-        in_specs=[smem] * 5,
-        out_specs=smem,
-        scratch_shapes=[pltpu.SMEM((row,), jnp.int32)],
-    )(targets, offsets.reshape(brick_count, views * 2), live, absorb_units, order)
+    longest = max(slots, brick_count * views)
+    size = (longest + LANES - 1) // LANES * LANES
     return pl.pallas_call(
         functools.partial(main_kernel, ny, nz, capacity),
         out_shape=jax.ShapeDtypeStruct((2, 4, extent, extent), F32),
-        in_specs=[smem, vmem, vmem, smem, smem, smem],
+        in_specs=[pl.BlockSpec(memory_space=pl.ANY), vmem, vmem, vmem, vmem, smem, smem, vmem, vmem],
         out_specs=vmem,
         scratch_shapes=[
+            pltpu.VMEM(bricks.shape, BF16),
             pltpu.VMEM((row, capacity, layers, extent, extent), BF16),
             pltpu.VMEM((row, capacity, layers, extent, extent), BF16),
             pltpu.VMEM((row, table_rows, LANES), jnp.int32),
-            pltpu.SMEM((row, table_rows, LANES), jnp.int32),
-            pltpu.VMEM((8, sort_size), jnp.int32),
-            pltpu.SMEM((8, sort_size), jnp.int32),
+            pltpu.VMEM((row, table_rows, LANES), jnp.int32),
+            pltpu.VMEM((LANES, LANES), jnp.int32),
+            pltpu.VMEM((size, LANES), jnp.int32),
+            pltpu.VMEM((8, size), jnp.int32),
+            pltpu.SMEM((8, size), jnp.int32),
+            pltpu.VMEM((size, LANES), F32),
+            pltpu.SMEM((size, LANES), F32),
+            pltpu.VMEM((8, size), jnp.int32),
+            pltpu.SMEM((8, size), jnp.int32),
             pltpu.VMEM((extent, extent), F32),
             pltpu.VMEM((slots, 4, extent, extent), BF16),
-            pltpu.VMEM((sort_size, LANES), jnp.int32),
+            pltpu.VMEM((size, LANES), jnp.int32),
             pltpu.SemaphoreType.DMA((row,)),
             pltpu.SemaphoreType.DMA((row,)),
             pltpu.SemaphoreType.DMA((row,)),
             pltpu.SemaphoreType.DMA((row,)),
-            pltpu.SemaphoreType.DMA((2,)),
+            pltpu.SemaphoreType.DMA((4,)),
         ],
         compiler_params=pltpu.CompilerParams(
             collective_id=0, has_side_effects=True, vmem_limit_bytes=48 * 1024 * 1024
         ),
-    )(table, table, bricks, shear, color_gain, color_bias)
+    )(
+        bricks, live.reshape(1, brick_count), shear, offsets, absorb.reshape(1, brick_count),
+        color_gain, color_bias, targets, order,
+    )
 
 
 def solution(mesh):

time: 71.5 us -> 64.9 us (0.908)
  Pallas kernels: 65.1 us -> 60.7 us
  local copies, waits for them, and re-layouts: 5.45 us -> 3.9 us
    pallas_call x1 -> x0, Pallas kernels: 3.28 us -> none  [body(): pl.pallas_call(functools.partial(table_kernel, row, capacity), out_shape=...]
    pallas_call x1, Pallas kernels: 61.8 us -> 60.7 us  [body(): pl.pallas_call(functools.partial(main_kernel, ny, nz, capacity), out_shap...]
    unnamed x17 -> x22, local copies, waits for them, and re-layouts: 4.8 us -> 3.9 us
where the time goes in v2:
time: 64.9 us; the launch traced here: 64.6 us
  Pallas kernels  60.7 us (94%)
  local copies, waits for them, and re-layouts  3.9 us (6%)
    pallas_call x1, Pallas kernels, body(): pl.pallas_call(functools.partial(main_kernel, ny, nz, capacity), out_shap...  60.7 us
    unnamed x22, local copies, waits for them, and re-layouts  3.9 us

profile of v2, /device:TPU:17, one launch (start us, length us, event | category | flops | bytes accessed | tf_op | source)
XLA Modules:
  0.0 64.6 jit_solution(4897289470864297136)
XLA Ops:
  0.0 0.0 copy-start.8
  0.0 0.0 copy-start.7
  0.0 0.7 %copy-done.8 = f32[4,2]{0,1:T(2,128)S(1)} copy-done((f32[4,2]{0,1:T(2,128)S(1)}, f32[4,2]{0,1:T(2,128)}, u32[]{:S(2)}) %copy-start.8) | copy-done | bytes 56
  0.7 0.0 copy-start.6
  0.7 0.1 copy.10.shear
  0.8 0.0 copy-done.7
  0.8 0.1 copy.12.targets
  0.9 0.5 copy-done.6
  1.4 0.0 copy-start.1
  1.4 0.0 copy-start.2
  1.4 0.0 copy-start.3
  1.4 0.0 copy-start.4
  1.4 0.0 copy-start.5
  1.4 0.1 copy.11.offsets
  1.5 0.6 copy-done.1
  2.0 0.0 copy-done.2
  2.1 0.0 copy-done.3
  2.1 0.0 copy-done.4
  2.1 0.0 copy-done.5
  2.1 0.0 copy-start
  2.1 1.0 %copy-done = bf16[8,2,128,128]{3,2,1,0:T(8,128)(2,1)S(1)} copy-done((bf16[8,2,128,128]{3,2,1,0:T(8,128)(2,1)S(1)}, bf16[8,2,128,128]{3,2,1,0:T(8,128)(2,1)}, u32[]{:S(2)}) %copy-start) | copy-done | bytes 524312
  3.1 60.7 %shard_map.91 = f32[2,4,128,128]{3,2,1,0:T(8,128)S(1)} custom-call(bf16[8,2,128,128]{3,2,1,0:T(8,128)(2,1)S(1)} %copy-done, s32[1,8]{1,0:T(1,128)S(1)} %bitcast.2, f32[4,2]{1,0:T(4,128)S(1)} %copy.10.shear, s32[8,4,2]{2,1,0:T(4,128)S(1)} %copy.11.offsets, bf16[1,8]{1,0:T(2,128)(2,1)S(1)} %bitcast.3, f32[3]{0:T(128)S(1)} %copy-done.4, f32[3]{0:T(128)S(1)} %copy-done.5, ...), custom_call_target="tpu_custom_call" | custom-call | tf_op jit(solution)/shard_map/pallas_call | solution.py:255
  63.8 0.8 %copy.14 = f32[2,4,128,128]{3,2,1,0:T(8,128)} copy(f32[2,4,128,128]{3,2,1,0:T(8,128)S(1)} %shard_map.91) | data formatting | bytes 1048576
Async XLA Ops:
  0.0 0.7 %copy-start.8 = (f32[4,2]{0,1:T(2,128)S(1)}, f32[4,2]{0,1:T(2,128)}, u32[]{:S(2)}) copy-start(f32[4,2]{0,1:T(2,128)} %param.11) | copy-start | bytes 100
  0.0 0.8 %copy-start.7 = (s32[8,4]{0,1:T(4,128)S(1)}, s32[8,4]{0,1:T(4,128)}, u32[]{:S(2)}) copy-start(s32[8,4]{0,1:T(4,128)} %param.16) | copy-start | bytes 388
  0.7 0.7 %copy-start.6 = (s32[8,4,2]{0,2,1:T(2,128)S(1)}, s32[8,4,2]{0,2,1:T(2,128)}, u32[]{:S(2)}) copy-start(s32[8,4,2]{0,2,1:T(2,128)} %param.12) | copy-start | bytes 772
  1.4 0.7 %copy-start.1 = (s32[4,8]{1,0:T(4,128)S(1)}, s32[4,8]{1,0:T(4,128)}, u32[]{:S(2)}) copy-start(s32[4,8]{1,0:T(4,128)} %order.1) | copy-start | bytes 388
  1.4 0.7 %copy-start.2 = (s32[8]{0:T(128)S(1)}, s32[8]{0:T(128)}, u32[]{:S(2)}) copy-start(s32[8]{0:T(128)} %param.10) | copy-start | bytes 100
  1.4 0.7 %copy-start.3 = (bf16[8]{0:T(256)(128)(2,1)S(1)}, bf16[8]{0:T(256)(128)(2,1)}, u32[]{:S(2)}) copy-start(bf16[8]{0:T(256)(128)(2,1)} %param.13) | copy-start | bytes 52
  1.4 0.7 %copy-start.4 = (f32[3]{0:T(128)S(1)}, f32[3]{0:T(128)}, u32[]{:S(2)}) copy-start(f32[3]{0:T(128)} %gain.1) | copy-start | bytes 40
  1.4 0.7 %copy-start.5 = (f32[3]{0:T(128)S(1)}, f32[3]{0:T(128)}, u32[]{:S(2)}) copy-start(f32[3]{0:T(128)} %bias.1) | copy-start | bytes 40
  2.1 1.0 %copy-start = (bf16[8,2,128,128]{3,2,1,0:T(8,128)(2,1)S(1)}, bf16[8,2,128,128]{3,2,1,0:T(8,128)(2,1)}, u32[]{:S(2)}) copy-start(bf16[8,2,128,128]{3,2,1,0:T(8,128)(2,1)} %bricks_in.1) | copy-start | bytes 1572868

commit v3 on v2

--- a/solution.py
+++ b/solution.py
@@ -19,9 +19,10 @@
     ny, nz, capacity,
     bricks_in, live, shear, offsets, absorb, gain, bias, targets, order,
     out,
-    bricks, send_buf, recv_buf, send_table, recv_table, raw, items, chosen_v, chosen_s,
+    bricks, raw_buf, relay_buf, raw_chosen_v, raw_chosen_s, send_buf, recv_buf, send_table, recv_table, raw, items, chosen_v, chosen_s,
     shift_v, shift_s, sort_v, sort_s, spacing, foot, keys,
-    table_send, table_recv, brick_send, brick_recv, local_sem,
+    table_send, table_recv, brick_send, brick_recv, raw_send, raw_recv, forward_send, relay_send,
+    local_sem,
 ):
     row = ny * nz
     slots = row * capacity
@@ -29,20 +30,34 @@
     views = targets.shape[1]
     size = keys.shape[0]
     my_y, my_z = lax.axis_index("gy"), lax.axis_index("gz")
-    steps = [(0, 0)] + [
-        (dy, dz)
-        for dz in sorted(range(nz), key=lambda dz: -min(dz, nz - dz))
-        for dy in range(ny)
-        if (dy, dz) != (0, 0)
-    ]
-
-    def peer(e):
-        dy, dz = steps[e]
+    half = nz // 2
+    relayed = nz >= 4
+    upper = my_z >= half
+    inner = (my_z == half) | (my_z == half - 1)
+    holder = inner | (my_z == half + 1) | (my_z == half - 2)
+
+    def mirror(dz):
+        return jnp.where(upper, dz, lax.rem(nz - dz, nz))
+
+    def leaves_raw(dz):
+        skip = mirror(dz)
+        return inner & ((skip == nz - 1) | (skip == nz - 2)) if relayed else False
+
+    def come(t):
+        if t == 0:
+            return jnp.int32(0)
+        first = {1: nz - 1, 2: 1}.get(t, t - 1)
+        return mirror(jnp.where(inner, first, t) if relayed else jnp.int32(t))
+
+    def go(t):
+        return mirror(jnp.where(inner, t, nz - t) if relayed else jnp.int32(t))
+
+    def peer(dy, dz):
         return lax.rem(my_y + dy, ny), lax.rem(my_z + dz, nz)
 
     barrier = pltpu.get_barrier_semaphore()
     for e in range(1, row):
-        py, pz = peer(e)
+        py, pz = peer(e % ny, e // ny)
         pl.semaphore_signal(barrier, inc=1, device_id={"gy": py, "gz": pz}, device_id_type=MESH)
 
     load_bricks = pltpu.make_async_copy(bricks_in, bricks, local_sem.at[0])
@@ -100,23 +115,74 @@
             device_id={"gy": py, "gz": pz}, device_id_type=MESH,
         )
 
-    def gather(e, py, pz, into):
+    def relay_copy(dy, dz, py, pz):
+        return pltpu.make_async_remote_copy(
+            src_ref=relay_buf.at[dy], dst_ref=recv_buf.at[dz * ny + dy],
+            send_sem=relay_send.at[dy], recv_sem=brick_recv.at[dz * ny + dy],
+            device_id={"gy": py, "gz": pz}, device_id_type=MESH,
+        )
+
+    def gather(source, chosen, py, pz, into, e):
         for c in range(capacity):
-            into[e, c] = bricks[chosen_s[0, (py * nz + pz) * capacity + c]]
+            into[e, c] = source[chosen[0, (py * nz + pz) * capacity + c]]
+
+    def send(dy, dz):
+        def direct():
+            e = dz * ny + dy
+            py, pz = peer(dy, dz)
+            gather(bricks, chosen_s, py, pz, send_buf, e)
+            brick_copy(e, py, pz).start()
+
+        if relayed:
+            pl.when(jnp.logical_not(leaves_raw(dz)))(direct)
+        else:
+            direct()
+
+    pieces = ny if count % ny == 0 else 1
+    depth = count // pieces
+    partner = 2 * half - 1 - my_z
+    beyond = jnp.where(upper, half + 1, half - 2)
+
+    def raw_copy(j, source, sent, pz):
+        part = pl.ds(j * depth, depth)
+        return pltpu.make_async_remote_copy(
+            src_ref=source.at[part], dst_ref=raw_buf.at[part],
+            send_sem=sent.at[j], recv_sem=raw_recv.at[j],
+            device_id={"gy": my_y, "gz": pz}, device_id_type=MESH,
+        )
+
+    def raw_chosen_copy(source, sent, pz):
+        return pltpu.make_async_remote_copy(
+            src_ref=source, dst_ref=raw_chosen_v,
+            send_sem=sent.at[pieces], recv_sem=raw_recv.at[pieces],
+            device_id={"gy": my_y, "gz": pz}, device_id_type=MESH,
+        )
 
     load_bricks.wait()
     load_chosen.wait()
-    gather(1, *peer(1), send_buf)
     pl.semaphore_wait(barrier, row - 1)
+    if relayed:
+        @pl.when(inner)
+        def _():
+            raw_copy(0, bricks, raw_send, partner).start()
+            raw_chosen_copy(chosen_v, raw_send, partner).start()
+
     for e in range(1, row):
-        table_copy(e, *peer(e)).start()
-    for e in range(1, row):
-        py, pz = peer(e)
-        if e > 1:
-            gather(e, py, pz, send_buf)
-        brick_copy(e, py, pz).start()
-
-    gather(0, my_y, my_z, recv_buf)
+        table_copy(e, *peer(e % ny, e // ny)).start()
+    for dy in range(ny):
+        send(dy, go(1))
+        if dy:
+            send(dy, jnp.int32(0))
+        if relayed and 0 < dy < pieces:
+            @pl.when(inner)
+            def _():
+                raw_copy(dy, bricks, raw_send, partner).start()
+
+    for t in range(2, nz):
+        for dy in range(ny):
+            send(dy, go(t))
+
+    gather(bricks, chosen_s, my_y, my_z, recv_buf, 0)
     recv_table[0] = send_table[my_y * nz + my_z]
     rows = lax.broadcasted_iota(jnp.int32, (extent, extent), 0)
     cols = lax.broadcasted_iota(jnp.int32, (extent, extent), 1)
@@ -190,21 +256,91 @@
                 foot[spot, n] = colors[n].astype(BF16)
             foot[spot, 3] = optical.astype(BF16)
 
-    render(0)
-
-    def arrived(e, _):
+    def arrived(e):
         brick_copy(e, my_y, my_z).wait_recv()
-        render(e)
-        return 0
-
-    lax.fori_loop(1, row, arrived, 0)
+
+    def plain(first, dz):
+        def step(dy, _):
+            arrived(dz * ny + dy)
+            render(dz * ny + dy)
+            return 0
+
+        lax.fori_loop(first, ny, step, 0)
+
+    render(jnp.int32(0))
+    plain(1, jnp.int32(0))
+    for t in range(1, nz):
+        dz = come(t)
+        if relayed and t == 1:
+            @pl.when(inner)
+            def _():
+                raw_chosen_copy(chosen_v, raw_send, partner).wait_recv()
+                raw_chosen_copy(raw_chosen_v, forward_send, beyond).start()
+
+            def step(dy, _):
+                @pl.when(inner & (dy < pieces))
+                def _():
+                    raw_copy(dy, bricks, raw_send, partner).wait_recv()
+                    raw_copy(dy, raw_buf, forward_send, beyond).start()
+
+                arrived(dz * ny + dy)
+                render(dz * ny + dy)
+                return 0
+
+            lax.fori_loop(0, ny, step, 0)
+        elif relayed and t == 2:
+            @pl.when(holder)
+            def _():
+                @pl.when(jnp.logical_not(inner))
+                def _():
+                    raw_chosen_copy(chosen_v, raw_send, partner).wait_recv()
+                    for j in range(pieces):
+                        raw_copy(j, bricks, raw_send, partner).wait_recv()
+
+                load_raw_chosen = pltpu.make_async_copy(raw_chosen_v, raw_chosen_s, local_sem.at[4])
+                load_raw_chosen.start()
+                load_raw_chosen.wait()
+                for dy in range(1, ny):
+                    py, pz = peer(dy, 0)
+                    gather(raw_buf, raw_chosen_s, py, pz, relay_buf, dy)
+                    relay_copy(dy, dz, py, pz).start()
+                gather(raw_buf, raw_chosen_s, my_y, my_z, recv_buf, dz * ny)
+
+            @pl.when(jnp.logical_not(holder))
+            def _():
+                arrived(dz * ny)
+
+            render(dz * ny)
+            plain(1, dz)
+        else:
+            plain(0, dz)
 
     def left(e, _):
         table_copy(e, my_y, my_z).wait_send()
-        brick_copy(e, my_y, my_z).wait_send()
+
+        def direct():
+            brick_copy(e, my_y, my_z).wait_send()
+
+        if relayed:
+            pl.when(jnp.logical_not(leaves_raw(lax.div(e, ny))))(direct)
+        else:
+            direct()
         return 0
 
     lax.fori_loop(1, row, left, 0)
+    if relayed:
+        @pl.when(inner)
+        def _():
+            for j in range(pieces):
+                raw_copy(j, bricks, raw_send, partner).wait_send()
+                raw_copy(j, raw_buf, forward_send, beyond).wait_send()
+            raw_chosen_copy(chosen_v, raw_send, partner).wait_send()
+            raw_chosen_copy(raw_chosen_v, forward_send, beyond).wait_send()
+
+        @pl.when(holder)
+        def _():
+            for dy in range(1, ny):
+                relay_copy(dy, jnp.int32(0), my_y, my_z).wait_send()
 
     height = 16
 
@@ -259,6 +395,10 @@
         out_specs=vmem,
         scratch_shapes=[
             pltpu.VMEM(bricks.shape, BF16),
+            pltpu.VMEM(bricks.shape, BF16),
+            pltpu.VMEM((ny, capacity, layers, extent, extent), BF16),
+            pltpu.VMEM((8, size), jnp.int32),
+            pltpu.SMEM((8, size), jnp.int32),
             pltpu.VMEM((row, capacity, layers, extent, extent), BF16),
             pltpu.VMEM((row, capacity, layers, extent, extent), BF16),
             pltpu.VMEM((row, table_rows, LANES), jnp.int32),
@@ -278,7 +418,11 @@
             pltpu.SemaphoreType.DMA((row,)),
             pltpu.SemaphoreType.DMA((row,)),
             pltpu.SemaphoreType.DMA((row,)),
-            pltpu.SemaphoreType.DMA((4,)),
+            pltpu.SemaphoreType.DMA((ny + 1,)),
+            pltpu.SemaphoreType.DMA((ny + 1,)),
+            pltpu.SemaphoreType.DMA((ny + 1,)),
+            pltpu.SemaphoreType.DMA((ny,)),
+            pltpu.SemaphoreType.DMA((5,)),
         ],
         compiler_params=pltpu.CompilerParams(
             collective_id=0, has_side_effects=True, vmem_limit_bytes=48 * 1024 * 1024

time: 64.9 us -> 64.3 us (level)
  the two profiles are of different devices: /device:TPU:17 before, /device:TPU:3 now
where the time goes in v3:
time: 64.3 us; the launch traced here: 64 us
  Pallas kernels  60.1 us (93%)
  local copies, waits for them, and re-layouts  3.9 us (6%)
    pallas_call x1, Pallas kernels, body(): pl.pallas_call(functools.partial(main_kernel, ny, nz, capacity), out_shap...  60.1 us
    unnamed x22, local copies, waits for them, and re-layouts  3.9 us

profile of v3, /device:TPU:3, one launch (start us, length us, event | category | flops | bytes accessed | tf_op | source)
XLA Modules:
  0.0 64.0 jit_solution(4085531351708696879)
XLA Ops:
  0.0 0.0 copy-start.8
  0.0 0.0 copy-start.7
  0.0 0.7 %copy-done.8 = f32[4,2]{0,1:T(2,128)S(1)} copy-done((f32[4,2]{0,1:T(2,128)S(1)}, f32[4,2]{0,1:T(2,128)}, u32[]{:S(2)}) %copy-start.8) | copy-done | bytes 56
  0.7 0.0 copy-start.6
  0.7 0.1 copy.10.shear
  0.8 0.0 copy-done.7
  0.8 0.1 copy.12.targets
  0.9 0.5 copy-done.6
  1.4 0.0 copy-start.1
  1.4 0.0 copy-start.2
  1.4 0.0 copy-start.3
  1.4 0.0 copy-start.4
  1.4 0.0 copy-start.5
  1.4 0.1 copy.11.offsets
  1.5 0.6 copy-done.1
  2.0 0.0 copy-done.2
  2.1 0.0 copy-done.3
  2.1 0.0 copy-done.4
  2.1 0.0 copy-done.5
  2.1 0.0 copy-start
  2.1 1.0 %copy-done = bf16[8,2,128,128]{3,2,1,0:T(8,128)(2,1)S(1)} copy-done((bf16[8,2,128,128]{3,2,1,0:T(8,128)(2,1)S(1)}, bf16[8,2,128,128]{3,2,1,0:T(8,128)(2,1)}, u32[]{:S(2)}) %copy-start) | copy-done | bytes 524312
  3.1 60.1 %shard_map.91 = f32[2,4,128,128]{3,2,1,0:T(8,128)S(1)} custom-call(bf16[8,2,128,128]{3,2,1,0:T(8,128)(2,1)S(1)} %copy-done, s32[1,8]{1,0:T(1,128)S(1)} %bitcast.2, f32[4,2]{1,0:T(4,128)S(1)} %copy.10.shear, s32[8,4,2]{2,1,0:T(4,128)S(1)} %copy.11.offsets, bf16[1,8]{1,0:T(2,128)(2,1)S(1)} %bitcast.3, f32[3]{0:T(128)S(1)} %copy-done.4, f32[3]{0:T(128)S(1)} %copy-done.5, ...), custom_call_target="tpu_custom_call" | custom-call | tf_op jit(solution)/shard_map/pallas_call | solution.py:391
  63.2 0.8 %copy.14 = f32[2,4,128,128]{3,2,1,0:T(8,128)} copy(f32[2,4,128,128]{3,2,1,0:T(8,128)S(1)} %shard_map.91) | data formatting | bytes 1048576
Async XLA Ops:
  0.0 0.7 %copy-start.8 = (f32[4,2]{0,1:T(2,128)S(1)}, f32[4,2]{0,1:T(2,128)}, u32[]{:S(2)}) copy-start(f32[4,2]{0,1:T(2,128)} %param.11) | copy-start | bytes 100
  0.0 0.8 %copy-start.7 = (s32[8,4]{0,1:T(4,128)S(1)}, s32[8,4]{0,1:T(4,128)}, u32[]{:S(2)}) copy-start(s32[8,4]{0,1:T(4,128)} %param.16) | copy-start | bytes 388
  0.7 0.7 %copy-start.6 = (s32[8,4,2]{0,2,1:T(2,128)S(1)}, s32[8,4,2]{0,2,1:T(2,128)}, u32[]{:S(2)}) copy-start(s32[8,4,2]{0,2,1:T(2,128)} %param.12) | copy-start | bytes 772
  1.4 0.7 %copy-start.1 = (s32[4,8]{1,0:T(4,128)S(1)}, s32[4,8]{1,0:T(4,128)}, u32[]{:S(2)}) copy-start(s32[4,8]{1,0:T(4,128)} %order.1) | copy-start | bytes 388
  1.4 0.7 %copy-start.2 = (s32[8]{0:T(128)S(1)}, s32[8]{0:T(128)}, u32[]{:S(2)}) copy-start(s32[8]{0:T(128)} %param.10) | copy-start | bytes 100
  1.4 0.7 %copy-start.3 = (bf16[8]{0:T(256)(128)(2,1)S(1)}, bf16[8]{0:T(256)(128)(2,1)}, u32[]{:S(2)}) copy-start(bf16[8]{0:T(256)(128)(2,1)} %param.13) | copy-start | bytes 52
  1.4 0.7 %copy-start.4 = (f32[3]{0:T(128)S(1)}, f32[3]{0:T(128)}, u32[]{:S(2)}) copy-start(f32[3]{0:T(128)} %gain.1) | copy-start | bytes 40
  1.4 0.7 %copy-start.5 = (f32[3]{0:T(128)S(1)}, f32[3]{0:T(128)}, u32[]{:S(2)}) copy-start(f32[3]{0:T(128)} %bias.1) | copy-start | bytes 40
  2.1 1.0 %copy-start = (bf16[8,2,128,128]{3,2,1,0:T(8,128)(2,1)S(1)}, bf16[8,2,128,128]{3,2,1,0:T(8,128)(2,1)}, u32[]{:S(2)}) copy-start(bf16[8,2,128,128]{3,2,1,0:T(8,128)(2,1)} %bricks_in.1) | copy-start | bytes 1572868

commit v4 on v3

--- a/solution.py
+++ b/solution.py
@@ -20,7 +20,7 @@
     bricks_in, live, shear, offsets, absorb, gain, bias, targets, order,
     out,
     bricks, raw_buf, relay_buf, raw_chosen_v, raw_chosen_s, send_buf, recv_buf, send_table, recv_table, raw, items, chosen_v, chosen_s,
-    shift_v, shift_s, sort_v, sort_s, spacing, foot, keys,
+    shift_v, shift_s, sort_v, sort_s, spacing, dense, foot, keys,
     table_send, table_recv, brick_send, brick_recv, raw_send, raw_recv, forward_send, relay_send,
     local_sem,
 ):
@@ -224,37 +224,42 @@
     to_shift.wait()
     to_sort.wait()
 
-    def interp(shifted):
-        return jnp.maximum(0.0, 1.0 - jnp.abs(spacing[...] - shifted)).astype(BF16)
+    def interp(distance):
+        return jnp.maximum(0.0, 1.0 - jnp.abs(distance)).astype(BF16)
+
+    strip_rows = 32
 
     def render(e):
+        spots = [e * capacity + c for c in range(capacity)]
         for c in range(capacity):
-            spot = e * capacity + c
-            optical, clear, colors = None, None, [None] * 3
             for k in range(layers):
-                across = interp(shift_s[spot, 3 * k])
-                downward = interp(shift_s[spot, 3 * k + 1])
+                across = interp(spacing[...] - shift_s[spots[c], 3 * k])
+                downward_t = interp(spacing[...] + shift_s[spots[c], 3 * k + 1])
                 halfway = jnp.dot(across, recv_buf[e, c, k], preferred_element_type=F32).astype(BF16)
-                density = lax.dot_general(
-                    halfway, downward, (((1,), (1,)), ((), ())), preferred_element_type=F32
-                )
-                rate = shift_s[spot, 3 * k + 2]
-                soft = jnp.maximum(density, 0.0) + jnp.log(1.0 + jnp.exp(-jnp.abs(density)))
-                thickness = rate * soft
-                passed = jnp.exp(-thickness)
-                half_alpha = 0.5 - 0.5 * passed
-                if k:
-                    half_alpha = half_alpha * clear
+                dense[c, k] = jnp.dot(halfway, downward_t, preferred_element_type=F32)
+        for c in range(capacity):
+            for begin in range(0, extent, strip_rows):
+                lines = slice(begin, begin + strip_rows)
+                optical, clear, colors = None, None, [None] * 3
+                for k in range(layers):
+                    density = dense[c, k, lines, :]
+                    rate = shift_s[spots[c], 3 * k + 2]
+                    soft = jnp.maximum(density, 0.0) + jnp.log(1.0 + jnp.exp(-jnp.abs(density)))
+                    thickness = rate * soft
+                    passed = jnp.exp(-thickness)
+                    half_alpha = 0.5 - 0.5 * passed
+                    if k:
+                        half_alpha = half_alpha * clear
+                    for n in range(3):
+                        lit = half_alpha + half_alpha * jnp.tanh(
+                            (0.5 * gain[n]) * density + 0.5 * bias[n]
+                        )
+                        colors[n] = lit if k == 0 else colors[n] + lit
+                    optical = thickness if k == 0 else optical + thickness
+                    clear = passed if k == 0 else clear * passed
                 for n in range(3):
-                    lit = half_alpha + half_alpha * jnp.tanh(
-                        (0.5 * gain[n]) * density + 0.5 * bias[n]
-                    )
-                    colors[n] = lit if k == 0 else colors[n] + lit
-                optical = thickness if k == 0 else optical + thickness
-                clear = passed if k == 0 else clear * passed
-            for n in range(3):
-                foot[spot, n] = colors[n].astype(BF16)
-            foot[spot, 3] = optical.astype(BF16)
+                    foot[spots[c], n, lines, :] = colors[n].astype(BF16)
+                foot[spots[c], 3, lines, :] = optical.astype(BF16)
 
     def arrived(e):
         brick_copy(e, my_y, my_z).wait_recv()
@@ -412,6 +417,7 @@
             pltpu.VMEM((8, size), jnp.int32),
             pltpu.SMEM((8, size), jnp.int32),
             pltpu.VMEM((extent, extent), F32),
+            pltpu.VMEM((capacity, layers, extent, extent), F32),
             pltpu.VMEM((slots, 4, extent, extent), BF16),
             pltpu.VMEM((size, LANES), jnp.int32),
             pltpu.SemaphoreType.DMA((row,)),

time: 64.3 us -> 63.7 us (level)
  no operation moved by 1% of the time
where the time goes in v4:
time: 63.7 us; the launch traced here: 63.4 us
  Pallas kernels  59.5 us (93%)
  local copies, waits for them, and re-layouts  3.9 us (6%)
    pallas_call x1, Pallas kernels, body(): pl.pallas_call(functools.partial(main_kernel, ny, nz, capacity), out_shap...  59.5 us
    unnamed x22, local copies, waits for them, and re-layouts  3.9 us

profile of v4, /device:TPU:3, one launch (start us, length us, event | category | flops | bytes accessed | tf_op | source)
XLA Modules:
  0.0 63.4 jit_solution(18110347002460350378)
XLA Ops:
  0.0 0.0 copy-start.8
  0.0 0.0 copy-start.7
  0.0 0.7 %copy-done.8 = f32[4,2]{0,1:T(2,128)S(1)} copy-done((f32[4,2]{0,1:T(2,128)S(1)}, f32[4,2]{0,1:T(2,128)}, u32[]{:S(2)}) %copy-start.8) | copy-done | bytes 56
  0.7 0.0 copy-start.6
  0.7 0.1 copy.10.shear
  0.8 0.0 copy-done.7
  0.8 0.1 copy.12.targets
  0.9 0.5 copy-done.6
  1.4 0.0 copy-start.1
  1.4 0.0 copy-start.2
  1.4 0.0 copy-start.3
  1.4 0.0 copy-start.4
  1.4 0.0 copy-start.5
  1.4 0.1 copy.11.offsets
  1.5 0.6 copy-done.1
  2.0 0.0 copy-done.2
  2.1 0.0 copy-done.3
  2.1 0.0 copy-done.4
  2.1 0.0 copy-done.5
  2.1 0.0 copy-start
  2.1 1.0 %copy-done = bf16[8,2,128,128]{3,2,1,0:T(8,128)(2,1)S(1)} copy-done((bf16[8,2,128,128]{3,2,1,0:T(8,128)(2,1)S(1)}, bf16[8,2,128,128]{3,2,1,0:T(8,128)(2,1)}, u32[]{:S(2)}) %copy-start) | copy-done | bytes 524312
  3.1 59.5 %shard_map.91 = f32[2,4,128,128]{3,2,1,0:T(8,128)S(1)} custom-call(bf16[8,2,128,128]{3,2,1,0:T(8,128)(2,1)S(1)} %copy-done, s32[1,8]{1,0:T(1,128)S(1)} %bitcast.2, f32[4,2]{1,0:T(4,128)S(1)} %copy.10.shear, s32[8,4,2]{2,1,0:T(4,128)S(1)} %copy.11.offsets, bf16[1,8]{1,0:T(2,128)(2,1)S(1)} %bitcast.3, f32[3]{0:T(128)S(1)} %copy-done.4, f32[3]{0:T(128)S(1)} %copy-done.5, ...), custom_call_target="tpu_custom_call" | custom-call | tf_op jit(solution)/shard_map/pallas_call | solution.py:396
  62.7 0.8 %copy.14 = f32[2,4,128,128]{3,2,1,0:T(8,128)} copy(f32[2,4,128,128]{3,2,1,0:T(8,128)S(1)} %shard_map.91) | data formatting | bytes 1048576
Async XLA Ops:
  0.0 0.7 %copy-start.8 = (f32[4,2]{0,1:T(2,128)S(1)}, f32[4,2]{0,1:T(2,128)}, u32[]{:S(2)}) copy-start(f32[4,2]{0,1:T(2,128)} %param.11) | copy-start | bytes 100
  0.0 0.8 %copy-start.7 = (s32[8,4]{0,1:T(4,128)S(1)}, s32[8,4]{0,1:T(4,128)}, u32[]{:S(2)}) copy-start(s32[8,4]{0,1:T(4,128)} %param.16) | copy-start | bytes 388
  0.7 0.7 %copy-start.6 = (s32[8,4,2]{0,2,1:T(2,128)S(1)}, s32[8,4,2]{0,2,1:T(2,128)}, u32[]{:S(2)}) copy-start(s32[8,4,2]{0,2,1:T(2,128)} %param.12) | copy-start | bytes 772
  1.4 0.7 %copy-start.1 = (s32[4,8]{1,0:T(4,128)S(1)}, s32[4,8]{1,0:T(4,128)}, u32[]{:S(2)}) copy-start(s32[4,8]{1,0:T(4,128)} %order.1) | copy-start | bytes 388
  1.4 0.7 %copy-start.2 = (s32[8]{0:T(128)S(1)}, s32[8]{0:T(128)}, u32[]{:S(2)}) copy-start(s32[8]{0:T(128)} %param.10) | copy-start | bytes 100
  1.4 0.7 %copy-start.3 = (bf16[8]{0:T(256)(128)(2,1)S(1)}, bf16[8]{0:T(256)(128)(2,1)}, u32[]{:S(2)}) copy-start(bf16[8]{0:T(256)(128)(2,1)} %param.13) | copy-start | bytes 52
  1.4 0.7 %copy-start.4 = (f32[3]{0:T(128)S(1)}, f32[3]{0:T(128)}, u32[]{:S(2)}) copy-start(f32[3]{0:T(128)} %gain.1) | copy-start | bytes 40
  1.4 0.7 %copy-start.5 = (f32[3]{0:T(128)S(1)}, f32[3]{0:T(128)}, u32[]{:S(2)}) copy-start(f32[3]{0:T(128)} %bias.1) | copy-start | bytes 40
  2.1 1.0 %copy-start = (bf16[8,2,128,128]{3,2,1,0:T(8,128)(2,1)S(1)}, bf16[8,2,128,128]{3,2,1,0:T(8,128)(2,1)}, u32[]{:S(2)}) copy-start(bf16[8,2,128,128]{3,2,1,0:T(8,128)(2,1)} %bricks_in.1) | copy-start | bytes 1572868

commit v5 on v2

--- a/solution.py
+++ b/solution.py
@@ -19,9 +19,10 @@
     ny, nz, capacity,
     bricks_in, live, shear, offsets, absorb, gain, bias, targets, order,
     out,
-    bricks, send_buf, recv_buf, send_table, recv_table, raw, items, chosen_v, chosen_s,
-    shift_v, shift_s, sort_v, sort_s, spacing, foot, keys,
-    table_send, table_recv, brick_send, brick_recv, local_sem,
+    bricks, column_v, column_s, send_buf, recv_buf, send_table, recv_table, raw, items, chosen_v, chosen_s,
+    shift_v, shift_s, sort_v, sort_s, spacing, dense, foot, keys,
+    table_send, table_recv, brick_send, brick_recv, column_send, column_recv, block_send, block_recv,
+    local_sem, *blocks,
 ):
     row = ny * nz
     slots = row * capacity
@@ -29,20 +30,24 @@
     views = targets.shape[1]
     size = keys.shape[0]
     my_y, my_z = lax.axis_index("gy"), lax.axis_index("gz")
-    steps = [(0, 0)] + [
-        (dy, dz)
-        for dz in sorted(range(nz), key=lambda dz: -min(dz, nz - dz))
-        for dy in range(ny)
-        if (dy, dz) != (0, 0)
-    ]
-
-    def peer(e):
-        dy, dz = steps[e]
+    way_to = (my_z + 1, my_z - 1)
+    has_next = (my_z + 1 < nz, my_z >= 1)
+
+    def exists(way, d):
+        return my_z >= d if way == 0 else my_z + d < nz
+
+    def step_of(way, d):
+        return d if way == 0 else nz - d
+
+    def held(way, d):
+        return blocks[way * (nz - 1) + d - 1] if d else bricks
+
+    def peer(dy, dz):
         return lax.rem(my_y + dy, ny), lax.rem(my_z + dz, nz)
 
     barrier = pltpu.get_barrier_semaphore()
     for e in range(1, row):
-        py, pz = peer(e)
+        py, pz = peer(e % ny, e // ny)
         pl.semaphore_signal(barrier, inc=1, device_id={"gy": py, "gz": pz}, device_id_type=MESH)
 
     load_bricks = pltpu.make_async_copy(bricks_in, bricks, local_sem.at[0])
@@ -100,23 +105,57 @@
             device_id={"gy": py, "gz": pz}, device_id_type=MESH,
         )
 
-    def gather(e, py, pz, into):
+    def gather(source, chosen, py, pz, into, e):
         for c in range(capacity):
-            into[e, c] = bricks[chosen_s[0, (py * nz + pz) * capacity + c]]
+            into[e, c] = source[chosen[(py * nz + pz) * capacity + c]]
+
+    pieces = ny if count % ny == 0 else 1
+    depth = count // pieces
+
+    def block_copy(way, d, j):
+        part = pl.ds(j * depth, depth)
+        return pltpu.make_async_remote_copy(
+            src_ref=held(way, d).at[part], dst_ref=held(way, d + 1).at[part],
+            send_sem=block_send.at[(way * nz + d) * pieces + j],
+            recv_sem=block_recv.at[(way * nz + d + 1) * pieces + j],
+            device_id={"gy": my_y, "gz": way_to[way]}, device_id_type=MESH,
+        )
+
+    def column_copy(dz, pz):
+        return pltpu.make_async_remote_copy(
+            src_ref=chosen_v, dst_ref=column_v.at[dz],
+            send_sem=column_send.at[dz], recv_sem=column_recv.at[dz],
+            device_id={"gy": my_y, "gz": pz}, device_id_type=MESH,
+        )
+
+    def offer(way, d, j):
+        @pl.when(exists(way, d) & has_next[way])
+        def _():
+            block_copy(way, d, j).start()
+
+    def share(block, chosen, dz, dy):
+        py, pz = peer(dy, 0)
+        gather(block, chosen, py, pz, send_buf, dz * ny + dy)
+        brick_copy(dz * ny + dy, py, pz).start()
 
     load_bricks.wait()
     load_chosen.wait()
-    gather(1, *peer(1), send_buf)
     pl.semaphore_wait(barrier, row - 1)
+    for way in range(2):
+        offer(way, 0, 0)
+    for dz in range(1, nz):
+        column_copy(dz, lax.rem(my_z + dz, nz)).start()
     for e in range(1, row):
-        table_copy(e, *peer(e)).start()
-    for e in range(1, row):
-        py, pz = peer(e)
-        if e > 1:
-            gather(e, py, pz, send_buf)
-        brick_copy(e, py, pz).start()
-
-    gather(0, my_y, my_z, recv_buf)
+        table_copy(e, *peer(e % ny, e // ny)).start()
+    for j in range(1, max(ny, pieces)):
+        if j < pieces:
+            for way in range(2):
+                offer(way, 0, j)
+        if j < ny:
+            share(bricks, chosen_s.at[0], 0, j)
+
+    gather(bricks, chosen_s.at[0], my_y, my_z, recv_buf, 0)
+    column_v[0] = chosen_v[...]
     recv_table[0] = send_table[my_y * nz + my_z]
     rows = lax.broadcasted_iota(jnp.int32, (extent, extent), 0)
     cols = lax.broadcasted_iota(jnp.int32, (extent, extent), 1)
@@ -127,6 +166,10 @@
         return 0
 
     lax.fori_loop(1, row, table_arrived, 0)
+    for dz in range(1, nz):
+        column_copy(dz, my_z).wait_recv()
+    load_column = pltpu.make_async_copy(column_v, column_s, local_sem.at[4])
+    load_column.start()
     keys[...] = jnp.full(keys.shape, -1, jnp.int32)
     for e in range(row):
         keys[e * capacity:(e + 1) * capacity, :] = recv_table[e, 0:capacity, :]
@@ -157,54 +200,96 @@
     to_sort.start()
     to_shift.wait()
     to_sort.wait()
-
-    def interp(shifted):
-        return jnp.maximum(0.0, 1.0 - jnp.abs(spacing[...] - shifted)).astype(BF16)
+    load_column.wait()
+
+    def interp(distance):
+        return jnp.maximum(0.0, 1.0 - jnp.abs(distance)).astype(BF16)
+
+    strip_rows = 32
 
     def render(e):
+        spots = [e * capacity + c for c in range(capacity)]
         for c in range(capacity):
-            spot = e * capacity + c
-            optical, clear, colors = None, None, [None] * 3
             for k in range(layers):
-                across = interp(shift_s[spot, 3 * k])
-                downward = interp(shift_s[spot, 3 * k + 1])
+                across = interp(spacing[...] - shift_s[spots[c], 3 * k])
+                downward_t = interp(spacing[...] + shift_s[spots[c], 3 * k + 1])
                 halfway = jnp.dot(across, recv_buf[e, c, k], preferred_element_type=F32).astype(BF16)
-                density = lax.dot_general(
-                    halfway, downward, (((1,), (1,)), ((), ())), preferred_element_type=F32
-                )
-                rate = shift_s[spot, 3 * k + 2]
-                soft = jnp.maximum(density, 0.0) + jnp.log(1.0 + jnp.exp(-jnp.abs(density)))
-                thickness = rate * soft
-                passed = jnp.exp(-thickness)
-                half_alpha = 0.5 - 0.5 * passed
-                if k:
-                    half_alpha = half_alpha * clear
+                dense[c, k] = jnp.dot(halfway, downward_t, preferred_element_type=F32)
+        for c in range(capacity):
+            for begin in range(0, extent, strip_rows):
+                lines = slice(begin, begin + strip_rows)
+                optical, clear, colors = None, None, [None] * 3
+                for k in range(layers):
+                    density = dense[c, k, lines, :]
+                    rate = shift_s[spots[c], 3 * k + 2]
+                    soft = jnp.maximum(density, 0.0) + jnp.log(1.0 + jnp.exp(-jnp.abs(density)))
+                    thickness = rate * soft
+                    passed = jnp.exp(-thickness)
+                    half_alpha = 0.5 - 0.5 * passed
+                    if k:
+                        half_alpha = half_alpha * clear
+                    for n in range(3):
+                        lit = half_alpha + half_alpha * jnp.tanh(
+                            (0.5 * gain[n]) * density + 0.5 * bias[n]
+                        )
+                        colors[n] = lit if k == 0 else colors[n] + lit
+                    optical = thickness if k == 0 else optical + thickness
+                    clear = passed if k == 0 else clear * passed
                 for n in range(3):
-                    lit = half_alpha + half_alpha * jnp.tanh(
-                        (0.5 * gain[n]) * density + 0.5 * bias[n]
-                    )
-                    colors[n] = lit if k == 0 else colors[n] + lit
-                optical = thickness if k == 0 else optical + thickness
-                clear = passed if k == 0 else clear * passed
-            for n in range(3):
-                foot[spot, n] = colors[n].astype(BF16)
-            foot[spot, 3] = optical.astype(BF16)
-
-    render(0)
-
-    def arrived(e, _):
-        brick_copy(e, my_y, my_z).wait_recv()
-        render(e)
-        return 0
-
-    lax.fori_loop(1, row, arrived, 0)
+                    foot[spots[c], n, lines, :] = colors[n].astype(BF16)
+                foot[spots[c], 3, lines, :] = optical.astype(BF16)
+
+    for d in range(nz):
+        below = exists(0, d)
+        number = jnp.int32(1) if d == 0 else below.astype(jnp.int32) + exists(1, d).astype(jnp.int32)
+
+        def entry(i, _):
+            if d + 1 < nz:
+                for way in range(2):
+                    @pl.when(exists(way, d + 1) & (i < pieces))
+                    def _():
+                        block_copy(way, d, i).wait_recv()
+                        if d + 2 < nz:
+                            offer(way, d + 1, i)
+
+            dz = jnp.where((i < ny) & below, d, nz - d)
+            e = dz * ny + lax.rem(i, ny)
+
+            @pl.when(lax.rem(i, ny) > 0)
+            def _():
+                brick_copy(e, my_y, my_z).wait_recv()
+
+            render(e)
+            return 0
+
+        lax.fori_loop(0, number * ny, entry, 0)
+        if d + 1 < nz:
+            for way in range(2):
+                @pl.when(exists(way, d + 1))
+                def _():
+                    dz = step_of(way, d + 1)
+                    for dy in range(1, ny):
+                        share(held(way, d + 1), column_s.at[dz, 0], dz, dy)
+                    gather(held(way, d + 1), column_s.at[dz, 0], my_y, my_z, recv_buf, dz * ny)
 
     def left(e, _):
         table_copy(e, my_y, my_z).wait_send()
-        brick_copy(e, my_y, my_z).wait_send()
+
+        @pl.when(lax.rem(e, ny) > 0)
+        def _():
+            brick_copy(e, my_y, my_z).wait_send()
+
         return 0
 
     lax.fori_loop(1, row, left, 0)
+    for dz in range(1, nz):
+        column_copy(dz, my_z).wait_send()
+    for way in range(2):
+        for d in range(nz - 1):
+            @pl.when(exists(way, d) & has_next[way])
+            def _():
+                for j in range(pieces):
+                    block_copy(way, d, j).wait_send()
 
     height = 16
 
@@ -259,6 +344,8 @@
         out_specs=vmem,
         scratch_shapes=[
             pltpu.VMEM(bricks.shape, BF16),
+            pltpu.VMEM((nz, 8, size), jnp.int32),
+            pltpu.SMEM((nz, 8, size), jnp.int32),
             pltpu.VMEM((row, capacity, layers, extent, extent), BF16),
             pltpu.VMEM((row, capacity, layers, extent, extent), BF16),
             pltpu.VMEM((row, table_rows, LANES), jnp.int32),
@@ -272,13 +359,19 @@
             pltpu.VMEM((8, size), jnp.int32),
             pltpu.SMEM((8, size), jnp.int32),
             pltpu.VMEM((extent, extent), F32),
+            pltpu.VMEM((capacity, layers, extent, extent), F32),
             pltpu.VMEM((slots, 4, extent, extent), BF16),
             pltpu.VMEM((size, LANES), jnp.int32),
             pltpu.SemaphoreType.DMA((row,)),
             pltpu.SemaphoreType.DMA((row,)),
             pltpu.SemaphoreType.DMA((row,)),
             pltpu.SemaphoreType.DMA((row,)),
-            pltpu.SemaphoreType.DMA((4,)),
+            pltpu.SemaphoreType.DMA((nz,)),
+            pltpu.SemaphoreType.DMA((nz,)),
+            pltpu.SemaphoreType.DMA((2 * nz * ny,)),
+            pltpu.SemaphoreType.DMA((2 * nz * ny,)),
+            pltpu.SemaphoreType.DMA((5,)),
+            *[pltpu.VMEM(bricks.shape, BF16) for _ in range(2 * (nz - 1))],
         ],
         compiler_params=pltpu.CompilerParams(
             collective_id=0, has_side_effects=True, vmem_limit_bytes=48 * 1024 * 1024

time: 64.9 us -> 58.7 us (0.904)
  the two profiles are of different devices: /device:TPU:17 before, /device:TPU:3 now
where the time goes in v5:
time: 58.7 us; the launch traced here: 57.6 us
  Pallas kernels  53.7 us (91%)
  local copies, waits for them, and re-layouts  3.9 us (7%)
    pallas_call x1, Pallas kernels, body(): pl.pallas_call(functools.partial(main_kernel, ny, nz, capacity), out_shap...  53.7 us
    unnamed x22, local copies, waits for them, and re-layouts  3.9 us

profile of v5, /device:TPU:3, one launch (start us, length us, event | category | flops | bytes accessed | tf_op | source)
XLA Modules:
  0.0 57.6 jit_solution(852780369440053684)
XLA Ops:
  0.0 0.0 copy-start.8
  0.0 0.0 copy-start.7
  0.0 0.7 %copy-done.8 = f32[4,2]{0,1:T(2,128)S(1)} copy-done((f32[4,2]{0,1:T(2,128)S(1)}, f32[4,2]{0,1:T(2,128)}, u32[]{:S(2)}) %copy-start.8) | copy-done | bytes 56
  0.7 0.0 copy-start.6
  0.7 0.1 copy.10.shear
  0.8 0.0 copy-done.7
  0.8 0.1 copy.12.targets
  0.9 0.5 copy-done.6
  1.4 0.0 copy-start.1
  1.4 0.0 copy-start.2
  1.4 0.0 copy-start.3
  1.4 0.0 copy-start.4
  1.4 0.0 copy-start.5
  1.4 0.1 copy.11.offsets
  1.5 0.6 copy-done.1
  2.0 0.0 copy-done.2
  2.1 0.0 copy-done.3
  2.1 0.0 copy-done.4
  2.1 0.0 copy-done.5
  2.1 0.0 copy-start
  2.1 1.0 %copy-done = bf16[8,2,128,128]{3,2,1,0:T(8,128)(2,1)S(1)} copy-done((bf16[8,2,128,128]{3,2,1,0:T(8,128)(2,1)S(1)}, bf16[8,2,128,128]{3,2,1,0:T(8,128)(2,1)}, u32[]{:S(2)}) %copy-start) | copy-done | bytes 524312
  3.1 53.7 %shard_map.91 = f32[2,4,128,128]{3,2,1,0:T(8,128)S(1)} custom-call(bf16[8,2,128,128]{3,2,1,0:T(8,128)(2,1)S(1)} %copy-done, s32[1,8]{1,0:T(1,128)S(1)} %bitcast.2, f32[4,2]{1,0:T(4,128)S(1)} %copy.10.shear, s32[8,4,2]{2,1,0:T(4,128)S(1)} %copy.11.offsets, bf16[1,8]{1,0:T(2,128)(2,1)S(1)} %bitcast.3, f32[3]{0:T(128)S(1)} %copy-done.4, f32[3]{0:T(128)S(1)} %copy-done.5, ...), custom_call_target="tpu_custom_call" | custom-call | tf_op jit(solution)/shard_map/pallas_call | solution.py:340
  56.8 0.8 %copy.14 = f32[2,4,128,128]{3,2,1,0:T(8,128)} copy(f32[2,4,128,128]{3,2,1,0:T(8,128)S(1)} %shard_map.91) | data formatting | bytes 1048576
Async XLA Ops:
  0.0 0.7 %copy-start.8 = (f32[4,2]{0,1:T(2,128)S(1)}, f32[4,2]{0,1:T(2,128)}, u32[]{:S(2)}) copy-start(f32[4,2]{0,1:T(2,128)} %param.11) | copy-start | bytes 100
  0.0 0.8 %copy-start.7 = (s32[8,4]{0,1:T(4,128)S(1)}, s32[8,4]{0,1:T(4,128)}, u32[]{:S(2)}) copy-start(s32[8,4]{0,1:T(4,128)} %param.16) | copy-start | bytes 388
  0.7 0.7 %copy-start.6 = (s32[8,4,2]{0,2,1:T(2,128)S(1)}, s32[8,4,2]{0,2,1:T(2,128)}, u32[]{:S(2)}) copy-start(s32[8,4,2]{0,2,1:T(2,128)} %param.12) | copy-start | bytes 772
  1.4 0.7 %copy-start.1 = (s32[4,8]{1,0:T(4,128)S(1)}, s32[4,8]{1,0:T(4,128)}, u32[]{:S(2)}) copy-start(s32[4,8]{1,0:T(4,128)} %order.1) | copy-start | bytes 388
  1.4 0.7 %copy-start.2 = (s32[8]{0:T(128)S(1)}, s32[8]{0:T(128)}, u32[]{:S(2)}) copy-start(s32[8]{0:T(128)} %param.10) | copy-start | bytes 100
  1.4 0.7 %copy-start.3 = (bf16[8]{0:T(256)(128)(2,1)S(1)}, bf16[8]{0:T(256)(128)(2,1)}, u32[]{:S(2)}) copy-start(bf16[8]{0:T(256)(128)(2,1)} %param.13) | copy-start | bytes 52
  1.4 0.7 %copy-start.4 = (f32[3]{0:T(128)S(1)}, f32[3]{0:T(128)}, u32[]{:S(2)}) copy-start(f32[3]{0:T(128)} %gain.1) | copy-start | bytes 40
  1.4 0.7 %copy-start.5 = (f32[3]{0:T(128)S(1)}, f32[3]{0:T(128)}, u32[]{:S(2)}) copy-start(f32[3]{0:T(128)} %bias.1) | copy-start | bytes 40
  2.1 1.0 %copy-start = (bf16[8,2,128,128]{3,2,1,0:T(8,128)(2,1)S(1)}, bf16[8,2,128,128]{3,2,1,0:T(8,128)(2,1)}, u32[]{:S(2)}) copy-start(bf16[8,2,128,128]{3,2,1,0:T(8,128)(2,1)} %bricks_in.1) | copy-start | bytes 1572868

commit v6 on v5

--- a/solution.py
+++ b/solution.py
@@ -17,17 +17,17 @@
 
 def main_kernel(
     ny, nz, capacity,
-    bricks_in, live, shear, offsets, absorb, gain, bias, targets, order,
+    bricks_in, live_in, shear_in, offsets_in, absorb_in, gain, bias, targets_in, order_in,
     out,
     bricks, column_v, column_s, send_buf, recv_buf, send_table, recv_table, raw, items, chosen_v, chosen_s,
     shift_v, shift_s, sort_v, sort_s, spacing, dense, foot, keys,
     table_send, table_recv, brick_send, brick_recv, column_send, column_recv, block_send, block_recv,
-    local_sem, *blocks,
+    far_buf, far_send, local_sem, live, shear, offsets, absorb, targets, order, *blocks,
 ):
     row = ny * nz
     slots = row * capacity
-    count, layers, extent, _ = bricks.shape
-    views = targets.shape[1]
+    count, layers, extent, _ = bricks_in.shape
+    views = targets_in.shape[1]
     size = keys.shape[0]
     my_y, my_z = lax.axis_index("gy"), lax.axis_index("gz")
     way_to = (my_z + 1, my_z - 1)
@@ -39,6 +39,8 @@
     def step_of(way, d):
         return d if way == 0 else nz - d
 
+    whole = nz - 1 if nz >= 3 else nz
+
     def held(way, d):
         return blocks[way * (nz - 1) + d - 1] if d else bricks
 
@@ -51,7 +53,18 @@
         pl.semaphore_signal(barrier, inc=1, device_id={"gy": py, "gz": pz}, device_id_type=MESH)
 
     load_bricks = pltpu.make_async_copy(bricks_in, bricks, local_sem.at[0])
+    loads = [
+        pltpu.make_async_copy(source, into, local_sem.at[5 + n])
+        for n, (source, into) in enumerate((
+            (live_in, live), (shear_in, shear), (offsets_in, offsets),
+            (absorb_in, absorb), (targets_in, targets), (order_in, order),
+        ))
+    ]
+    for load in loads:
+        load.start()
     load_bricks.start()
+    for load in loads:
+        load.wait()
 
     raw[...] = jnp.zeros(raw.shape, jnp.int32)
     raw[0:views, 0:count] = order[...]
@@ -128,6 +141,21 @@
             device_id={"gy": my_y, "gz": pz}, device_id_type=MESH,
         )
 
+    def far_copy(way, dy, py):
+        place = step_of(way, nz - 1) * ny + dy
+        return pltpu.make_async_remote_copy(
+            src_ref=far_buf.at[way * ny + dy], dst_ref=recv_buf.at[place],
+            send_sem=far_send.at[way * ny + dy], recv_sem=brick_recv.at[place],
+            device_id={"gy": py, "gz": way_to[way]}, device_id_type=MESH,
+        )
+
+    def far(way):
+        for dy in range(ny):
+            py = lax.rem(my_y + dy, ny)
+            chosen = column_s.at[step_of(way, nz - 2), 0]
+            gather(held(way, nz - 2), chosen, py, way_to[way], far_buf, way * ny + dy)
+            far_copy(way, dy, py).start()
+
     def offer(way, d, j):
         @pl.when(exists(way, d) & has_next[way])
         def _():
@@ -244,18 +272,34 @@
         number = jnp.int32(1) if d == 0 else below.astype(jnp.int32) + exists(1, d).astype(jnp.int32)
 
         def entry(i, _):
-            if d + 1 < nz:
+            if d + 1 < whole:
                 for way in range(2):
                     @pl.when(exists(way, d + 1) & (i < pieces))
                     def _():
                         block_copy(way, d, i).wait_recv()
-                        if d + 2 < nz:
+                        if d + 2 < whole:
                             offer(way, d + 1, i)
+
+                @pl.when(i == pieces - 1)
+                def _():
+                    for way in range(2):
+                        if d + 2 == whole and whole < nz:
+                            @pl.when(exists(way, d + 1) & has_next[way])
+                            def _():
+                                far(way)
+
+                    for way in range(2):
+                        @pl.when(exists(way, d + 1))
+                        def _():
+                            dz = step_of(way, d + 1)
+                            for dy in range(1, ny):
+                                share(held(way, d + 1), column_s.at[dz, 0], dz, dy)
+                            gather(held(way, d + 1), column_s.at[dz, 0], my_y, my_z, recv_buf, dz * ny)
 
             dz = jnp.where((i < ny) & below, d, nz - d)
             e = dz * ny + lax.rem(i, ny)
 
-            @pl.when(lax.rem(i, ny) > 0)
+            @pl.when((lax.rem(i, ny) > 0) | (d >= whole))
             def _():
                 brick_copy(e, my_y, my_z).wait_recv()
 
@@ -263,19 +307,17 @@
             return 0
 
         lax.fori_loop(0, number * ny, entry, 0)
-        if d + 1 < nz:
-            for way in range(2):
-                @pl.when(exists(way, d + 1))
-                def _():
-                    dz = step_of(way, d + 1)
-                    for dy in range(1, ny):
-                        share(held(way, d + 1), column_s.at[dz, 0], dz, dy)
-                    gather(held(way, d + 1), column_s.at[dz, 0], my_y, my_z, recv_buf, dz * ny)
 
     def left(e, _):
         table_copy(e, my_y, my_z).wait_send()
 
-        @pl.when(lax.rem(e, ny) > 0)
+        sent = lax.rem(e, ny) > 0
+        if whole < nz:
+            dz = lax.div(e, ny)
+            first, last = (my_z == 0) & (dz == 1), (my_z == nz - 1) & (dz == nz - 1)
+            sent = sent & jnp.logical_not(first | last)
+
+        @pl.when(sent)
         def _():
             brick_copy(e, my_y, my_z).wait_send()
 
@@ -285,11 +327,16 @@
     for dz in range(1, nz):
         column_copy(dz, my_z).wait_send()
     for way in range(2):
-        for d in range(nz - 1):
+        for d in range(whole - 1):
             @pl.when(exists(way, d) & has_next[way])
             def _():
                 for j in range(pieces):
                     block_copy(way, d, j).wait_send()
+        if whole < nz:
+            @pl.when(exists(way, whole - 1) & has_next[way])
+            def _():
+                for dy in range(ny):
+                    far_copy(way, dy, my_y).wait_send()
 
     height = 16
 
@@ -334,13 +381,15 @@
     slots = row * capacity
     smem = pl.BlockSpec(memory_space=pltpu.SMEM)
     vmem = pl.BlockSpec(memory_space=pltpu.VMEM)
+    hbm = pl.BlockSpec(memory_space=pltpu.HBM)
+    live_row, absorb_row = live.reshape(1, brick_count), absorb.reshape(1, brick_count)
     table_rows = (capacity + 7) // 8 * 8
     longest = max(slots, brick_count * views)
     size = (longest + LANES - 1) // LANES * LANES
     return pl.pallas_call(
         functools.partial(main_kernel, ny, nz, capacity),
         out_shape=jax.ShapeDtypeStruct((2, 4, extent, extent), F32),
-        in_specs=[pl.BlockSpec(memory_space=pl.ANY), vmem, vmem, vmem, vmem, smem, smem, vmem, vmem],
+        in_specs=[hbm, hbm, hbm, hbm, hbm, smem, smem, hbm, hbm],
         out_specs=vmem,
         scratch_shapes=[
             pltpu.VMEM(bricks.shape, BF16),
@@ -370,14 +419,20 @@
             pltpu.SemaphoreType.DMA((nz,)),
             pltpu.SemaphoreType.DMA((2 * nz * ny,)),
             pltpu.SemaphoreType.DMA((2 * nz * ny,)),
-            pltpu.SemaphoreType.DMA((5,)),
+            pltpu.VMEM((2 * ny, capacity, layers, extent, extent), BF16),
+            pltpu.SemaphoreType.DMA((2 * ny,)),
+            pltpu.SemaphoreType.DMA((11,)),
+            *[
+                pltpu.VMEM(a.shape, a.dtype)
+                for a in (live_row, shear, offsets, absorb_row, targets, order)
+            ],
             *[pltpu.VMEM(bricks.shape, BF16) for _ in range(2 * (nz - 1))],
         ],
         compiler_params=pltpu.CompilerParams(
             collective_id=0, has_side_effects=True, vmem_limit_bytes=48 * 1024 * 1024
         ),
     )(
-        bricks, live.reshape(1, brick_count), shear, offsets, absorb.reshape(1, brick_count),
+        bricks, live_row, shear, offsets, absorb_row,
         color_gain, color_bias, targets, order,
     )
 

time: 58.7 us -> 53.7 us (0.915)
  the two profiles are of different devices: /device:TPU:3 before, /device:TPU:1 now
where the time goes in v6:
time: 53.7 us; the launch traced here: 53.5 us
  Pallas kernels  49.6 us (92%)
  local copies, waits for them, and re-layouts  3.9 us (7%)
    pallas_call x1, Pallas kernels, body(): pl.pallas_call(functools.partial(main_kernel, ny, nz, capacity), out_shap...  49.6 us
    unnamed x22, local copies, waits for them, and re-layouts  3.9 us

profile of v6, /device:TPU:1, one launch (start us, length us, event | category | flops | bytes accessed | tf_op | source)
XLA Modules:
  0.0 53.5 jit_solution(13018775221637309447)
XLA Ops:
  0.0 0.0 copy-start.8
  0.0 0.0 copy-start.7
  0.0 0.7 %copy-done.8 = f32[4,2]{0,1:T(2,128)S(1)} copy-done((f32[4,2]{0,1:T(2,128)S(1)}, f32[4,2]{0,1:T(2,128)}, u32[]{:S(2)}) %copy-start.8) | copy-done | bytes 56
  0.7 0.0 copy-start.6
  0.7 0.1 copy.10.shear_in
  0.8 0.0 copy-done.7
  0.8 0.1 copy.12.targets_in
  0.9 0.5 copy-done.6
  1.4 0.0 copy-start.1
  1.4 0.0 copy-start.2
  1.4 0.0 copy-start.3
  1.4 0.0 copy-start.4
  1.4 0.0 copy-start.5
  1.4 0.1 copy.11.offsets_in
  1.5 0.6 %copy-done.1 = s32[4,8]{1,0:T(4,128)S(1)} copy-done((s32[4,8]{1,0:T(4,128)S(1)}, s32[4,8]{1,0:T(4,128)}, u32[]{:S(2)}) %copy-start.1) | copy-done | bytes 152
  2.0 0.0 copy-done.2
  2.1 0.0 copy-done.3
  2.1 0.0 copy-done.4
  2.1 0.0 copy-done.5
  2.1 0.0 copy-start
  2.1 1.0 %copy-done = bf16[8,2,128,128]{3,2,1,0:T(8,128)(2,1)S(1)} copy-done((bf16[8,2,128,128]{3,2,1,0:T(8,128)(2,1)S(1)}, bf16[8,2,128,128]{3,2,1,0:T(8,128)(2,1)}, u32[]{:S(2)}) %copy-start) | copy-done | bytes 524312
  3.1 49.6 %shard_map.91 = f32[2,4,128,128]{3,2,1,0:T(8,128)S(1)} custom-call(bf16[8,2,128,128]{3,2,1,0:T(8,128)(2,1)S(1)} %copy-done, s32[1,8]{1,0:T(1,128)S(1)} %bitcast.2, f32[4,2]{1,0:T(4,128)S(1)} %copy.10.shear_in, s32[8,4,2]{2,1,0:T(4,128)S(1)} %copy.11.offsets_in, bf16[1,8]{1,0:T(2,128)(2,1)S(1)} %bitcast.3, f32[3]{0:T(128)S(1)} %copy-done.4, f32[3]{0:T(128)S(1)} %copy-done.5, ...), custom_call_target="tpu_custom_call" | custom-call | tf_op jit(solution)/shard_map/pallas_call | solution.py:389
  52.7 0.8 %copy.14 = f32[2,4,128,128]{3,2,1,0:T(8,128)} copy(f32[2,4,128,128]{3,2,1,0:T(8,128)S(1)} %shard_map.91) | data formatting | bytes 1048576
Async XLA Ops:
  0.0 0.7 %copy-start.8 = (f32[4,2]{0,1:T(2,128)S(1)}, f32[4,2]{0,1:T(2,128)}, u32[]{:S(2)}) copy-start(f32[4,2]{0,1:T(2,128)} %param.11) | copy-start | bytes 100
  0.0 0.8 %copy-start.7 = (s32[8,4]{0,1:T(4,128)S(1)}, s32[8,4]{0,1:T(4,128)}, u32[]{:S(2)}) copy-start(s32[8,4]{0,1:T(4,128)} %param.16) | copy-start | bytes 388
  0.7 0.7 %copy-start.6 = (s32[8,4,2]{0,2,1:T(2,128)S(1)}, s32[8,4,2]{0,2,1:T(2,128)}, u32[]{:S(2)}) copy-start(s32[8,4,2]{0,2,1:T(2,128)} %param.12) | copy-start | bytes 772
  1.4 0.7 %copy-start.1 = (s32[4,8]{1,0:T(4,128)S(1)}, s32[4,8]{1,0:T(4,128)}, u32[]{:S(2)}) copy-start(s32[4,8]{1,0:T(4,128)} %order_in.1) | copy-start | bytes 388
  1.4 0.7 %copy-start.2 = (s32[8]{0:T(128)S(1)}, s32[8]{0:T(128)}, u32[]{:S(2)}) copy-start(s32[8]{0:T(128)} %param.10) | copy-start | bytes 100
  1.4 0.7 %copy-start.3 = (bf16[8]{0:T(256)(128)(2,1)S(1)}, bf16[8]{0:T(256)(128)(2,1)}, u32[]{:S(2)}) copy-start(bf16[8]{0:T(256)(128)(2,1)} %param.13) | copy-start | bytes 52
  1.4 0.7 %copy-start.4 = (f32[3]{0:T(128)S(1)}, f32[3]{0:T(128)}, u32[]{:S(2)}) copy-start(f32[3]{0:T(128)} %gain.1) | copy-start | bytes 40
  1.4 0.7 %copy-start.5 = (f32[3]{0:T(128)S(1)}, f32[3]{0:T(128)}, u32[]{:S(2)}) copy-start(f32[3]{0:T(128)} %bias.1) | copy-start | bytes 40
  2.1 1.0 %copy-start = (bf16[8,2,128,128]{3,2,1,0:T(8,128)(2,1)S(1)}, bf16[8,2,128,128]{3,2,1,0:T(8,128)(2,1)}, u32[]{:S(2)}) copy-start(bf16[8,2,128,128]{3,2,1,0:T(8,128)(2,1)} %bricks_in.1) | copy-start | bytes 1572868

commit v7 on v6

--- a/solution.py
+++ b/solution.py
@@ -27,7 +27,7 @@
     row = ny * nz
     slots = row * capacity
     count, layers, extent, _ = bricks_in.shape
-    views = targets_in.shape[1]
+    views = targets_in.shape[0]
     size = keys.shape[0]
     my_y, my_z = lax.axis_index("gy"), lax.axis_index("gz")
     way_to = (my_z + 1, my_z - 1)
@@ -68,18 +68,22 @@
 
     raw[...] = jnp.zeros(raw.shape, jnp.int32)
     raw[0:views, 0:count] = order[...]
-    raw[views:views + 1, 0:count] = live[...]
+    raw[views:2 * views, 0:count] = targets[...]
+    for v in range(views):
+        raw[2 * views + 2 * v:2 * views + 2 * v + 2, 0:count] = offsets[v]
+    raw[4 * views:4 * views + 1, 0:count] = live[...]
     units = jnp.round(absorb[...].astype(F32) * ABSORB_UNIT)
-    raw[views + 1:views + 2, 0:count] = units.astype(jnp.int32)
+    raw[4 * views + 1:4 * views + 2, 0:count] = units.astype(jnp.int32)
     turned = raw[...].T
     items[...] = jnp.zeros(items.shape, jnp.int32)
     for v in range(views):
         mine = slice(v * count, (v + 1) * count)
-        items[mine, OFF_X:OFF_Y + 1] = offsets[:, v, :]
-        items[mine, LIVE:LIVE + 1] = turned[0:count, views:views + 1]
+        at = 2 * views + 2 * v
+        items[mine, OFF_X:OFF_Y + 1] = turned[0:count, at:at + 2]
+        items[mine, LIVE:LIVE + 1] = turned[0:count, 4 * views:4 * views + 1]
         items[mine, VIEW:VIEW + 1] = jnp.full((count, 1), v, jnp.int32)
-        items[mine, ABSORB:ABSORB + 1] = turned[0:count, views + 1:views + 2]
-        items[mine, TILE:TILE + 1] = targets[:, v:v + 1]
+        items[mine, ABSORB:ABSORB + 1] = turned[0:count, 4 * views + 1:4 * views + 2]
+        items[mine, TILE:TILE + 1] = turned[0:count, views + v:views + v + 1]
         items[mine, RANK:RANK + 1] = turned[0:count, v:v + 1]
         items[mine, BRICK:BRICK + 1] = lax.broadcasted_iota(jnp.int32, (count, 1), 0)
     me = lax.broadcasted_iota(jnp.int32, (size, size), 0)
@@ -205,7 +209,7 @@
     for axis in range(2):
         slope = jnp.zeros((size, 1), F32)
         for v in range(views):
-            slope = jnp.where(view == v, shear[v:v + 1, axis:axis + 1], slope)
+            slope = jnp.where(view == v, shear[axis:axis + 1, v:v + 1], slope)
         offset = keys[:, OFF_X + axis:OFF_X + axis + 1].astype(F32)
         for k in range(layers):
             shift_v[:, 3 * k + axis:3 * k + axis + 1] = offset + float(k - layers // 2) * slope
@@ -375,13 +379,14 @@
 
 def body(ny, nz, bricks, live, shear, offsets, absorb, color_gain, color_bias, targets, order):
     brick_count, layers, extent, _ = bricks.shape
-    views = shear.shape[0]
+    views = targets.shape[1]
     row = ny * nz
     capacity = (brick_count * views + row - 1) // row
     slots = row * capacity
     smem = pl.BlockSpec(memory_space=pltpu.SMEM)
     vmem = pl.BlockSpec(memory_space=pltpu.VMEM)
     hbm = pl.BlockSpec(memory_space=pltpu.HBM)
+    shear, offsets, targets = shear.T, offsets.transpose(1, 2, 0), targets.T
     live_row, absorb_row = live.reshape(1, brick_count), absorb.reshape(1, brick_count)
     table_rows = (capacity + 7) // 8 * 8
     longest = max(slots, brick_count * views)
@@ -429,7 +434,7 @@
             *[pltpu.VMEM(bricks.shape, BF16) for _ in range(2 * (nz - 1))],
         ],
         compiler_params=pltpu.CompilerParams(
-            collective_id=0, has_side_effects=True, vmem_limit_bytes=48 * 1024 * 1024
+            collective_id=0, has_side_effects=True, vmem_limit_bytes=60 * 1024 * 1024
         ),
     )(
         bricks, live_row, shear, offsets, absorb_row,

time: 53.7 us -> 52.5 us (0.978)
  the two profiles are of different devices: /device:TPU:1 before, /device:TPU:3 now
where the time goes in v7:
time: 52.5 us; the launch traced here: 51.5 us
  Pallas kernels  49.6 us (94%)
  local copies, waits for them, and re-layouts  1.87 us (4%)
    pallas_call x1, Pallas kernels, body(): pl.pallas_call(functools.partial(main_kernel, ny, nz, capacity), out_shap...  49.6 us
    unnamed x1, local copies, waits for them, and re-layouts  1.87 us

profile of v7, /device:TPU:3, one launch (start us, length us, event | category | flops | bytes accessed | tf_op | source)
XLA Modules:
  0.0 51.5 jit_solution(4523254366899685633)
XLA Ops:
  0.0 49.6 %shard_map.91 = f32[2,4,128,128]{3,2,1,0:T(8,128)} custom-call(bf16[8,2,128,128]{3,2,1,0:T(8,128)(2,1)} %bricks_in.1, s32[1,8]{1,0:T(1,128)} %bitcast.8, f32[2,4]{1,0:T(2,128)} %bitcast.7, s32[4,2,8]{2,1,0:T(2,128)} %bitcast.5, bf16[1,8]{1,0:T(2,128)(2,1)} %bitcast.9, f32[3]{0:T(128)} %gain.1, f32[3]{0:T(128)} %bias.1, s32[4,8]{1,0:T(4,128)} %bitcast.6, ...), custom_call_target="tpu_custom_call" | custom-call | tf_op jit(solution)/shard_map/pallas_call | solution.py:394
  49.7 1.9 %copy.11 = f32[2,4,128,128]{3,2,1,0:T(8,128)} copy(f32[2,4,128,128]{3,2,1,0:T(8,128)} %shard_map.91) | data formatting | bytes 1048576

commit v8 on v7

--- a/solution.py
+++ b/solution.py
@@ -365,7 +365,7 @@
 
         zero = jnp.zeros((height, extent), F32)
         optical0, optical1, color0, color1 = lax.fori_loop(
-            0, slots, visit, (zero, zero, (zero,) * 3, (zero,) * 3), unroll=4
+            0, slots, visit, (zero, zero, (zero,) * 3, (zero,) * 3), unroll=8
         )
         for n in range(3):
             out[0, n, lines, :] = color0[n]

time: 52.5 us -> 52.2 us (level)
  no operation moved by 1% of the time
where the time goes in v8:
time: 52.2 us; the launch traced here: 51.2 us
  Pallas kernels  49.3 us (94%)
  local copies, waits for them, and re-layouts  1.87 us (4%)
    pallas_call x1, Pallas kernels, body(): pl.pallas_call(functools.partial(main_kernel, ny, nz, capacity), out_shap...  49.3 us
    unnamed x1, local copies, waits for them, and re-layouts  1.87 us

profile of v8, /device:TPU:3, one launch (start us, length us, event | category | flops | bytes accessed | tf_op | source)
XLA Modules:
  0.0 51.2 jit_solution(18190726836553582701)
XLA Ops:
  0.0 49.3 %shard_map.91 = f32[2,4,128,128]{3,2,1,0:T(8,128)} custom-call(bf16[8,2,128,128]{3,2,1,0:T(8,128)(2,1)} %bricks_in.1, s32[1,8]{1,0:T(1,128)} %bitcast.8, f32[2,4]{1,0:T(2,128)} %bitcast.7, s32[4,2,8]{2,1,0:T(2,128)} %bitcast.5, bf16[1,8]{1,0:T(2,128)(2,1)} %bitcast.9, f32[3]{0:T(128)} %gain.1, f32[3]{0:T(128)} %bias.1, s32[4,8]{1,0:T(4,128)} %bitcast.6, ...), custom_call_target="tpu_custom_call" | custom-call | tf_op jit(solution)/shard_map/pallas_call | solution.py:394
  49.3 1.9 %copy.11 = f32[2,4,128,128]{3,2,1,0:T(8,128)} copy(f32[2,4,128,128]{3,2,1,0:T(8,128)} %shard_map.91) | data formatting | bytes 1048576
